TPU v7x, 32 devices: a whole 2x2x4 slice. The times are simulated.
32 devices in a mesh: ctx: 8 (over z, y), head: 4 (over x, core).
Axes of the slice: x: 2, y: 2, z: 4, core: 2. Of those that a mesh axis runs over, the one named last changes fastest.
Arguments:
- query: bfloat16 [4096, 1024], P(('ctx', 'head')), may hold values from -7 to 7
- key: bfloat16 [4096, 1024], P(('ctx', 'head')), may hold values from -7 to 7
- value: bfloat16 [4096, 1024], P(('ctx', 'head')), may hold values from -6 to 6
- grad_out: bfloat16 [4096, 1024], P(('ctx', 'head')), may hold values from -6 to 6
- neighbour: int32 [32, 8], replicated, may hold values from 0 to 31, as said below
- counts: int32 [32], replicated, may hold values from 1 to 8, as said below
Outputs:
- attn_out: bfloat16 [4096, 1024], P(('ctx', 'head'))
- grad_query: bfloat16 [4096, 1024], P(('ctx', 'head'))
- grad_key: bfloat16 [4096, 1024], P(('ctx', 'head'))
- grad_value: bfloat16 [4096, 1024], P(('ctx', 'head'))
Inputs may be any that keep to these rules, and one draw needn't show every extreme that they name: `neighbour`: row b lists key blocks for query block b: its first entry is b itself, and every entry lies within 8 blocks of b in the periodic block order; some row has an entry exactly 8 blocks ahead, and some row one exactly that far behind. Query block b uses the first counts[b] slots of its row; some block uses all 8 slots and some only one.
All inputs are finite; a program needn't handle non-finite values.
Results may differ from a plain program's by a relative error of at most 0.0083.
Values may be sent and summed in bfloat16 or wider, within the bound.
A program may use at most 64 MiB of HBM per device.

v0:
```python
import functools
import math

import jax
import jax.numpy as jnp
from jax import lax
from jax.experimental import pallas as pl
from jax.experimental.pallas import tpu as pltpu
from jax.sharding import PartitionSpec as P

H = 16
E = 64
BLK = 128
NNB = 8
REACH = 2


def passed_along(value, axis, steps):
    count = lax.axis_size(axis)
    pairs = [(source, (source + steps) % count) for source in range(count)]
    return lax.ppermute(value, axis, pairs)


def group_rows(blocks_shard, block_len):
    limit = max(512 // block_len, 1)
    best = 1
    for candidate in range(1, blocks_shard + 1):
        if blocks_shard % candidate == 0 and candidate <= limit:
            best = candidate
    return best


def on_device_windowed(query, key, value, grad_out, neighbour, counts):
    tok_rows = query.shape[0]
    groups = lax.axis_size("head")
    per_dev = H // groups
    head_cols = per_dev * E
    moved = (
        lax.all_to_all(
            query.reshape(tok_rows, groups, head_cols),
            "head",
            split_axis=1,
            concat_axis=0,
            tiled=True,
        ),
        lax.all_to_all(
            key.reshape(tok_rows, groups, head_cols),
            "head",
            split_axis=1,
            concat_axis=0,
            tiled=True,
        ),
        lax.all_to_all(
            value.reshape(tok_rows, groups, head_cols),
            "head",
            split_axis=1,
            concat_axis=0,
            tiled=True,
        ),
        lax.all_to_all(
            grad_out.reshape(tok_rows, groups, head_cols),
            "head",
            split_axis=1,
            concat_axis=0,
            tiled=True,
        ),
    )
    shard_rows = groups * tok_rows
    query_s = moved[0].reshape(shard_rows, head_cols)
    key_s = moved[1].reshape(shard_rows, head_cols)
    value_s = moved[2].reshape(shard_rows, head_cols)
    grad_s = moved[3].reshape(shard_rows, head_cols)
    paired = jnp.concatenate([key_s, value_s], axis=1)
    cycle_len = lax.axis_size("ctx")
    position = lax.axis_index("ctx")
    blocks_shard = shard_rows // BLK
    all_blocks = blocks_shard * cycle_len
    fetched = {}
    offsets_all = list(range(1, REACH + 1)) + [-offset for offset in range(1, REACH + 1)]
    for offset in offsets_all:
        fetched[offset] = passed_along(paired, "ctx", offset)
    ordered = (
        [fetched[REACH - place] for place in range(REACH)]
        + [paired]
        + [fetched[-(place + 1)] for place in range(REACH)]
    )
    span_shards = 2 * REACH + 1
    window = jnp.concatenate(ordered, axis=0).reshape(
        span_shards * blocks_shard, BLK, 2 * head_cols
    )
    rows_nbr = lax.dynamic_slice_in_dim(neighbour, position * blocks_shard, blocks_shard, 0)
    local_idx = jnp.mod(rows_nbr - (position - REACH) * blocks_shard, all_blocks)
    used = lax.dynamic_slice_in_dim(counts, position * blocks_shard, blocks_shard, 0)
    per_group = group_rows(blocks_shard, BLK)
    turns = blocks_shard // per_group
    scale_factor = 1.0 / math.sqrt(E)
    query_g = query_s.reshape(turns, per_group, BLK, per_dev, E)
    grad_g = grad_s.reshape(turns, per_group, BLK, per_dev, E)
    index_g = local_idx.reshape(turns, per_group, NNB)
    used_g = used.reshape(turns, per_group)

    def one_group(totals, inputs):
        queries, cotangent, chosen, used_now = inputs
        selected = window[chosen]
        keys_sel = selected[..., :head_cols].reshape(per_group, NNB, BLK, per_dev, E)
        values_sel = selected[..., head_cols:].reshape(per_group, NNB, BLK, per_dev, E)
        usable = jnp.arange(NNB)[None, :] < used_now[:, None]
        allowed = usable[:, None, None, :, None]
        scores = (
            jnp.einsum("rihe,rjthe->rhijt", queries, keys_sel, preferred_element_type=jnp.float32)
            * scale_factor
        )
        masked = jnp.where(allowed, scores, -1e30)
        highest = jnp.max(masked, axis=(3, 4), keepdims=True)
        raised = jnp.where(allowed, jnp.exp(masked - highest), 0.0)
        total = jnp.sum(raised, axis=(3, 4), keepdims=True)
        probability = raised / total
        weights = probability.astype(jnp.bfloat16)
        out_rows = jnp.einsum(
            "rhijt,rjthe->rihe", weights, values_sel, preferred_element_type=jnp.float32
        ).astype(jnp.bfloat16)
        dprob = jnp.einsum(
            "rihe,rjthe->rhijt", cotangent, values_sel, preferred_element_type=jnp.float32
        )
        row_delta = jnp.sum(probability * dprob, axis=(3, 4), keepdims=True)
        dscore = (probability * (dprob - row_delta) * scale_factor).astype(jnp.bfloat16)
        dquery = jnp.einsum(
            "rhijt,rjthe->rihe", dscore, keys_sel, preferred_element_type=jnp.float32
        ).astype(jnp.bfloat16)
        dkey_part = jnp.einsum(
            "rhijt,rihe->rjthe", dscore, queries, preferred_element_type=jnp.float32
        )
        dvalue_part = jnp.einsum(
            "rhijt,rihe->rjthe", weights, cotangent, preferred_element_type=jnp.float32
        )
        joined = jnp.concatenate(
            [
                dkey_part.reshape(per_group * NNB, BLK, head_cols),
                dvalue_part.reshape(per_group * NNB, BLK, head_cols),
            ],
            axis=-1,
        )
        totals = totals.at[chosen.reshape(-1)].add(joined)
        return (totals, (out_rows, dquery))

    start_grads = jnp.zeros((span_shards * blocks_shard, BLK, 2 * head_cols), jnp.float32)
    grads_window, results = lax.scan(one_group, start_grads, (query_g, grad_g, index_g, used_g))
    grads_window = grads_window.reshape(span_shards, shard_rows, 2 * head_cols)
    combined = grads_window[REACH]
    offsets_back = list(range(1, REACH + 1)) + [-offset for offset in range(1, REACH + 1)]
    for offset in offsets_back:
        combined = combined + passed_along(
            grads_window[REACH - offset].astype(jnp.bfloat16), "ctx", -offset
        ).astype(jnp.float32)
    combined = combined.astype(jnp.bfloat16)
    dkey_s = combined[:, :head_cols]
    dvalue_s = combined[:, head_cols:]
    out_s = results[0].reshape(shard_rows, head_cols)
    dquery_s = results[1].reshape(shard_rows, head_cols)
    back = (
        lax.all_to_all(
            out_s.reshape(shard_rows, 1, head_cols), "head", split_axis=0, concat_axis=1, tiled=True
        ),
        lax.all_to_all(
            dquery_s.reshape(shard_rows, 1, head_cols),
            "head",
            split_axis=0,
            concat_axis=1,
            tiled=True,
        ),
        lax.all_to_all(
            dkey_s.reshape(shard_rows, 1, head_cols),
            "head",
            split_axis=0,
            concat_axis=1,
            tiled=True,
        ),
        lax.all_to_all(
            dvalue_s.reshape(shard_rows, 1, head_cols),
            "head",
            split_axis=0,
            concat_axis=1,
            tiled=True,
        ),
    )
    width = groups * head_cols
    return (
        back[0].reshape(tok_rows, width),
        back[1].reshape(tok_rows, width),
        back[2].reshape(tok_rows, width),
        back[3].reshape(tok_rows, width),
    )


MESH_ID = pl.DeviceIdType.MESH
F32 = jnp.float32
BF16 = jnp.bfloat16
VMEM_BYTES = 20 * 1024 * 1024


def place_of():
    index = lax.axis_index("ctx") * lax.axis_size("head") + lax.axis_index("head")
    return lax.div(index, 2), lax.rem(index, 2)


def device_of(owner, side):
    n_head = lax.axis_size("head")
    index = 2 * owner + side
    return (lax.div(index, n_head), lax.rem(index, n_head))


def partners(pairs, owner, step):
    half = pairs // 2
    far = 1 - lax.div(step, half)
    base = lax.rem(lax.div(owner, half) + far, 2) * half
    low, turn = lax.rem(owner, half), lax.rem(step, half)
    return base + lax.rem(low + turn, half), base + lax.rem(low - turn + half, half)


def each_step(pairs, body):
    def one(step, carry):
        body(step)
        return carry

    lax.fori_loop(0, pairs // 2, one, 0)
    lax.fori_loop(pairs // 2 + 1, pairs, one, 0)


def greet(pairs):
    owner, side = place_of()
    barrier = pltpu.get_barrier_semaphore()
    pl.semaphore_signal(barrier, inc=1, device_id=device_of(owner, 1 - side), device_id_type=MESH_ID)

    def one(step):
        to, _ = partners(pairs, owner, step)
        pl.semaphore_signal(barrier, inc=1, device_id=device_of(to, side), device_id_type=MESH_ID)

    each_step(pairs, one)
    return barrier


def spread_kernel(
    pairs, query, key, value, grad_out, qd, kv, kvt, own_rows, send_qd, send_kv,
    load, qd_out, qd_in, kv_out, kv_in, share_out, share_in,
):
    owner, side = place_of()
    loads = [
        pltpu.make_async_copy(array, own_rows.at[place], load.at[place])
        for place, array in enumerate((key, value, query, grad_out))
    ]
    for copy in loads:
        copy.start()
    barrier = greet(pairs)

    def pack(first, pieces):
        loads[first].wait()
        loads[first + 1].wait()
        for pair in range(pairs // 2):
            cols = slice(2 * E * pair, 2 * E * (pair + 1))
            a = own_rows[first, :, cols]
            b = own_rows[first + 1, :, cols]
            pieces[2 * pair] = jnp.concatenate([a[:, :E], b[:, :E]], axis=1)
            pieces[2 * pair + 1] = jnp.concatenate([a[:, E:], b[:, E:]], axis=1)

    def kv_copy(step, to, source):
        return pltpu.make_async_remote_copy(
            src_ref=send_kv.at[to],
            dst_ref=kv.at[2 * source + side],
            send_sem=kv_out.at[step],
            recv_sem=kv_in.at[step],
            device_id=device_of(to, side),
            device_id_type=MESH_ID,
        )

    def qd_copy(step, to, source):
        return pltpu.make_async_remote_copy(
            src_ref=send_qd.at[to],
            dst_ref=qd.at[source],
            send_sem=qd_out.at[step],
            recv_sem=qd_in.at[step],
            device_id=device_of(to, side),
            device_id_type=MESH_ID,
        )

    def share_copy(step, source, whose):
        return pltpu.make_async_remote_copy(
            src_ref=kv.at[2 * source + side],
            dst_ref=kv.at[2 * source + whose],
            send_sem=share_out.at[step],
            recv_sem=share_in.at[step],
            device_id=device_of(owner, 1 - side),
            device_id_type=MESH_ID,
        )

    def send_keys(step):
        to, _ = partners(pairs, owner, step)
        kv_copy(step, to, owner).start()

    def send_queries(step):
        to, _ = partners(pairs, owner, step)
        qd_copy(step, to, owner).start()

    pack(0, send_kv)
    pl.semaphore_wait(barrier, pairs)
    each_step(pairs, send_keys)
    pack(2, send_qd)
    each_step(pairs, send_queries)
    mine = 2 * owner + side
    kv[mine] = send_kv[owner]
    qd[owner] = send_qd[owner]
    share_copy(pairs // 2, owner, side).start()
    kvt[mine] = kv[mine].T

    def pass_on(step):
        _, source = partners(pairs, owner, step)
        kv_copy(step, owner, source).wait_recv()
        share_copy(step, source, side).start()
        kvt[2 * source + side] = kv[2 * source + side].T

    def take_share(step):
        _, source = partners(pairs, owner, step)
        share_copy(step, source, side).wait_send()
        share_copy(step, source, 1 - side).wait_recv()
        kvt[2 * source + 1 - side] = kv[2 * source + 1 - side].T

    def finish(step):
        to, source = partners(pairs, owner, step)
        qd_copy(step, owner, source).wait_recv()
        qd_copy(step, to, owner).wait_send()
        kv_copy(step, to, owner).wait_send()

    each_step(pairs, pass_on)
    take_share(jnp.int32(pairs // 2))
    each_step(pairs, take_share)
    each_step(pairs, finish)


def attend_kernel(
    blocks, neighbour_hbm, counts, qd, kv, kvt, od, totals, neighbour, pair_scr, x_scr, load
):
    _, side = place_of()
    half = blocks // 2
    scale = 1.0 / math.sqrt(E)
    exp_scale = scale * math.log2(math.e)
    low = lax.broadcasted_iota(jnp.int32, (BLK, 2 * E), 1) < E
    top = lax.broadcasted_iota(jnp.int32, (2 * E, BLK), 0) < E
    names_copy = pltpu.make_async_copy(neighbour_hbm, neighbour, load)
    names_copy.start()

    def clear(block, carry):
        totals[block] = jnp.zeros((BLK, 2 * E), F32)
        return carry

    lax.fori_loop(0, blocks, clear, 0)
    names_copy.wait()

    def folded(array, op):
        return op(array.reshape(BLK // 8, 8, BLK), axis=0)

    def rows_with(place, block, used):
        both = qd[place]
        zero = jnp.zeros_like(both)
        spread = jnp.concatenate([jnp.where(low, both, zero), jnp.where(low, zero, both)], axis=0)
        names = [neighbour[block, slot] for slot in range(used)]
        highest = None
        for slot in range(used):
            result = lax.dot_general(
                kv[names[slot]], spread, (((1,), (1,)), ((), ())), preferred_element_type=F32
            )
            pair_scr[slot] = result
            part = folded(result[:, :BLK], jnp.max)
            highest = part if highest is None else jnp.maximum(highest, part)
        highest = jnp.max(highest, axis=0, keepdims=True)
        total = jnp.zeros((8, BLK), F32)
        delta = jnp.zeros((8, BLK), F32)
        for slot in range(used):
            raised = jnp.exp2((pair_scr[slot, :, :BLK] - highest) * exp_scale)
            pair_scr[slot, :, :BLK] = raised
            total = total + folded(raised, jnp.sum)
            delta = delta + folded(raised * pair_scr[slot, :, BLK:], jnp.sum)
        inverse = 1.0 / jnp.sum(total, axis=0, keepdims=True)
        delta = jnp.sum(delta, axis=0, keepdims=True) * inverse
        for slot in range(used):
            probability = pair_scr[slot, :, :BLK] * inverse
            dscore = (probability * scale) * (pair_scr[slot, :, BLK:] - delta)
            x_scr[slot] = jnp.concatenate(
                [dscore.astype(BF16), probability.astype(BF16)], axis=1
            )
        rows = jnp.zeros((2 * E, 2 * BLK), F32)
        for slot in range(0, used, 2):
            if slot + 1 < used:
                keys_t = jnp.concatenate([kvt[names[slot]], kvt[names[slot + 1]]], axis=1)
                grads = jnp.concatenate([x_scr[slot], x_scr[slot + 1]], axis=0)
            else:
                keys_t = kvt[names[slot]]
                grads = x_scr[slot]
            rows = rows + jnp.dot(keys_t, grads, preferred_element_type=F32)
        for slot in range(used):
            totals[names[slot]] += jnp.dot(x_scr[slot], spread, preferred_element_type=F32)
        od[place] = jnp.where(top, rows[:, :BLK], rows[:, BLK:]).T.astype(BF16)

    def one_block(place, carry):
        block = 2 * place + side
        used_now = counts[block]
        for used in range(1, NNB + 1):
            pl.when(used_now == used)(functools.partial(rows_with, place, block, used))
        return carry

    lax.fori_loop(0, half, one_block, 0)


def collect_kernel(
    pairs, od, totals, got_od, got_kv, other, shared, send_kv,
    od_out, od_in, kv_out, kv_in, share_out, share_in,
):
    owner, side = place_of()
    barrier = greet(pairs)

    def share_copy(step, place):
        return pltpu.make_async_remote_copy(
            src_ref=other.at[place],
            dst_ref=shared.at[place],
            send_sem=share_out.at[step],
            recv_sem=share_in.at[step],
            device_id=device_of(owner, 1 - side),
            device_id_type=MESH_ID,
        )

    def od_copy(step, to, source):
        return pltpu.make_async_remote_copy(
            src_ref=od.at[to],
            dst_ref=got_od.at[source],
            send_sem=od_out.at[step],
            recv_sem=od_in.at[step],
            device_id=device_of(to, side),
            device_id_type=MESH_ID,
        )

    def kv_copy(step, to, source):
        return pltpu.make_async_remote_copy(
            src_ref=send_kv.at[to],
            dst_ref=got_kv.at[source],
            send_sem=kv_out.at[step],
            recv_sem=kv_in.at[step],
            device_id=device_of(to, side),
            device_id_type=MESH_ID,
        )

    def narrow(place, carry):
        other[place] = totals[2 * place + 1 - side].astype(BF16)
        return carry

    lax.fori_loop(0, pairs, narrow, 0)
    pl.semaphore_wait(barrier, pairs)

    def start_all(step):
        to, _ = partners(pairs, owner, step)
        od_copy(step, to, owner).start()
        share_copy(step, to).start()

    def summed(place):
        return (totals[2 * place + side] + shared[place].astype(F32)).astype(BF16)

    def add_and_send(step):
        to, _ = partners(pairs, owner, step)
        share_copy(step, to).wait_recv()
        send_kv[to] = summed(to)
        kv_copy(step, to, owner).start()

    def finish(step):
        to, source = partners(pairs, owner, step)
        od_copy(step, owner, source).wait_recv()
        kv_copy(step, owner, source).wait_recv()
        od_copy(step, to, owner).wait_send()
        kv_copy(step, to, owner).wait_send()
        share_copy(step, to).wait_send()

    each_step(pairs, start_all)
    share_copy(pairs // 2, owner).start()
    each_step(pairs, add_and_send)
    share_copy(pairs // 2, owner).wait_recv()
    got_kv[owner] = summed(owner)
    got_od[owner] = od[owner]
    each_step(pairs, finish)
    share_copy(pairs // 2, owner).wait_send()


def join_kernel(pairs, got_od, got_kv, out, dquery, dkey, dvalue, rows, store):
    copies = []
    for place, (pieces, part, array) in enumerate(
        ((got_od, 1, out), (got_od, 0, dquery), (got_kv, 0, dkey), (got_kv, 1, dvalue))
    ):
        cut = slice(part * E, (part + 1) * E)
        for pair in range(pairs // 2):
            cols = slice(2 * E * pair, 2 * E * (pair + 1))
            rows[place, :, cols] = jnp.concatenate(
                [pieces[2 * pair][:, cut], pieces[2 * pair + 1][:, cut]], axis=1
            )
        copies.append(pltpu.make_async_copy(rows.at[place], array, store.at[place]))
        copies[-1].start()
    for copy in copies:
        copy.wait()


def on_device_whole(query, key, value, grad_out, neighbour, counts):
    pairs = lax.axis_size("ctx") * lax.axis_size("head") // 2
    blocks = 2 * pairs
    width = query.shape[1]
    in_vmem = pl.BlockSpec(memory_space=pltpu.VMEM)
    in_smem = pl.BlockSpec(memory_space=pltpu.SMEM)
    in_hbm = pl.BlockSpec(memory_space=pltpu.HBM)
    many = pltpu.SemaphoreType.DMA((pairs,))
    piece = (BLK, 2 * E)
    own_pieces = jax.ShapeDtypeStruct((pairs, *piece), BF16)
    all_pieces = jax.ShapeDtypeStruct((blocks, *piece), BF16)
    with jax.named_scope("spread_heads"):
        qd, kv, kvt = pl.pallas_call(
            functools.partial(spread_kernel, pairs),
            out_shape=(own_pieces, all_pieces, all_pieces),
            in_specs=[in_hbm] * 4,
            out_specs=(in_vmem,) * 3,
            scratch_shapes=[pltpu.VMEM((4, BLK, width), BF16)]
            + [pltpu.VMEM((pairs, *piece), BF16)] * 2
            + [pltpu.SemaphoreType.DMA((4,))]
            + [many] * 6,
            compiler_params=pltpu.CompilerParams(
                collective_id=0, has_side_effects=True, vmem_limit_bytes=VMEM_BYTES
            ),
        )(query, key, value, grad_out)
    with jax.named_scope("block_attention"):
        od, totals = pl.pallas_call(
            functools.partial(attend_kernel, blocks),
            out_shape=(own_pieces, jax.ShapeDtypeStruct((blocks, *piece), F32)),
            in_specs=[in_hbm, in_smem] + [in_vmem] * 3,
            out_specs=(in_vmem,) * 2,
            scratch_shapes=[
                pltpu.SMEM(neighbour.shape, jnp.int32),
                pltpu.VMEM((NNB, BLK, 2 * BLK), F32),
                pltpu.VMEM((NNB, BLK, 2 * BLK), BF16),
                pltpu.SemaphoreType.DMA(()),
            ],
            compiler_params=pltpu.CompilerParams(vmem_limit_bytes=VMEM_BYTES),
        )(neighbour, counts, qd, kv, kvt)
    with jax.named_scope("collect_heads"):
        got_od, got_kv = pl.pallas_call(
            functools.partial(collect_kernel, pairs),
            out_shape=(own_pieces,) * 2,
            in_specs=[in_vmem] * 2,
            out_specs=(in_vmem,) * 2,
            scratch_shapes=[pltpu.VMEM((pairs, *piece), BF16)] * 3 + [many] * 6,
            compiler_params=pltpu.CompilerParams(
                collective_id=1, has_side_effects=True, vmem_limit_bytes=VMEM_BYTES
            ),
        )(od, totals)
    with jax.named_scope("join_heads"):
        return pl.pallas_call(
            functools.partial(join_kernel, pairs),
            out_shape=(jax.ShapeDtypeStruct((BLK, width), BF16),) * 4,
            in_specs=[in_vmem] * 2,
            out_specs=(in_hbm,) * 4,
            scratch_shapes=[
                pltpu.VMEM((4, BLK, width), BF16),
                pltpu.SemaphoreType.DMA((4,)),
            ],
            compiler_params=pltpu.CompilerParams(vmem_limit_bytes=VMEM_BYTES),
        )(got_od, got_kv)


def on_device(query, key, value, grad_out, neighbour, counts):
    devices = lax.axis_size("ctx") * lax.axis_size("head")
    if devices == 2 * H and query.shape == (BLK, H * E) and counts.shape[0] == devices:
        return on_device_whole(query, key, value, grad_out, neighbour, counts)
    return on_device_windowed(query, key, value, grad_out, neighbour, counts)


def solution(mesh):
    return jax.shard_map(
        on_device,
        mesh=mesh,
        in_specs=(
            P(("ctx", "head"), None),
            P(("ctx", "head"), None),
            P(("ctx", "head"), None),
            P(("ctx", "head"), None),
            P(),
            P(),
        ),
        out_specs=(
            P(("ctx", "head"), None),
            P(("ctx", "head"), None),
            P(("ctx", "head"), None),
            P(("ctx", "head"), None),
        ),
        check_vma=False,
    )
```

profile of v0, /device:TPU:0, one launch (start us, length us, event | category | flops | bytes accessed | tf_op | source)
XLA Modules:
  0.0 80.3 jit_solution(13014903493880513973)
XLA Ops:
  0.6 0.8 copy.10.neighbour_hbm
  1.4 0.0 copy-start
  1.4 0.9 %copy-done = bf16[128,1024]{1,0:T(8,128)(2,1)S(1)} copy-done((bf16[128,1024]{1,0:T(8,128)(2,1)S(1)}, bf16[128,1024]{1,0:T(8,128)(2,1)}, u32[]{:S(2)}) %copy-start) | copy-done | bytes 262168
  2.3 0.0 copy-start.1
  2.3 0.9 %copy-done.1 = bf16[128,1024]{1,0:T(8,128)(2,1)S(1)} copy-done((bf16[128,1024]{1,0:T(8,128)(2,1)S(1)}, bf16[128,1024]{1,0:T(8,128)(2,1)}, u32[]{:S(2)}) %copy-start.1) | copy-done | bytes 262168
  3.3 0.0 copy-start.2
  3.3 0.9 %copy-done.2 = bf16[128,1024]{1,0:T(8,128)(2,1)S(1)} copy-done((bf16[128,1024]{1,0:T(8,128)(2,1)S(1)}, bf16[128,1024]{1,0:T(8,128)(2,1)}, u32[]{:S(2)}) %copy-start.2) | copy-done | bytes 262168
  4.2 0.0 copy-start.3
  4.2 0.9 %copy-done.3 = bf16[128,1024]{1,0:T(8,128)(2,1)S(1)} copy-done((bf16[128,1024]{1,0:T(8,128)(2,1)S(1)}, bf16[128,1024]{1,0:T(8,128)(2,1)}, u32[]{:S(2)}) %copy-start.3) | copy-done | bytes 262168
  5.2 31.6 %spread_heads.1 = (bf16[16,128,128]{2,1,0:T(8,128)(2,1)S(1)}, bf16[32,128,128]{2,1,0:T(8,128)(2,1)S(1)}, bf16[32,128,128]{2,1,0:T(8,128)(2,1)S(1)}) custom-call(bf16[128,1024]{1,0:T(8,128)(2,1)S(1)} %copy-done, bf16[128,1024]{1,0:T(8,128)(2,1)S(1)} %copy-done.1, bf16[128,1024]{1,0:T(8,128)(2,1)S(1)} %copy-done.2, bf16[128,1024]{1,0:T(8,128)(2,1)S(1)} %copy-done.3), custom_call_target="tpu_custom_call" | custom-call | tf_op jit(solution)/shard_map/spread_heads/pallas_call | solution.py:517
  36.8 0.0 copy-start.4
  36.8 0.6 copy-done.4
  37.4 13.7 %block_attention.1 = (bf16[16,128,128]{2,1,0:T(8,128)(2,1)S(1)}, f32[32,128,128]{2,1,0:T(8,128)S(1)}) custom-call(s32[32,8]{1,0:T(8,128)S(1)} %copy.10.neighbour_hbm, s32[32]{0:T(128)S(1)} %copy-done.4, bf16[16,128,128]{2,1,0:T(8,128)(2,1)S(1)} %get-tuple-element.11.qd, bf16[32,128,128]{2,1,0:T(8,128)(2,1)S(1)} %get-tuple-element.12.kv, ...), custom_call_target="tpu_custom_call" | custom-call | tf_op jit(solution)/shard_map/block_attention/pallas_call | solution.py:531
  51.1 28.0 %collect_heads.1 = (bf16[16,128,128]{2,1,0:T(8,128)(2,1)S(1)}, bf16[16,128,128]{2,1,0:T(8,128)(2,1)S(1)}) custom-call(bf16[16,128,128]{2,1,0:T(8,128)(2,1)S(1)} %get-tuple-element.14.od, f32[32,128,128]{2,1,0:T(8,128)S(1)} %get-tuple-element.15.totals), custom_call_target="tpu_custom_call" | custom-call | tf_op jit(solution)/shard_map/collect_heads/pallas_call | solution.py:545
  79.2 1.1 %join_heads.1 = (bf16[128,1024]{1,0:T(8,128)(2,1)}, bf16[128,1024]{1,0:T(8,128)(2,1)}, bf16[128,1024]{1,0:T(8,128)(2,1)}, bf16[128,1024]{1,0:T(8,128)(2,1)}) custom-call(bf16[16,128,128]{2,1,0:T(8,128)(2,1)S(1)} %get-tuple-element.16.got_od, bf16[16,128,128]{2,1,0:T(8,128)(2,1)S(1)} %get-tuple-element.17.got_kv), custom_call_target="tpu_custom_call" | custom-call | tf_op jit(solution)/shard_map/join_heads/pallas_call | solution.py:556
Async XLA Ops:
  1.4 0.9 %copy-start = (bf16[128,1024]{1,0:T(8,128)(2,1)S(1)}, bf16[128,1024]{1,0:T(8,128)(2,1)}, u32[]{:S(2)}) copy-start(bf16[128,1024]{1,0:T(8,128)(2,1)} %query.1) | copy-start | bytes 786436
  2.3 0.9 %copy-start.1 = (bf16[128,1024]{1,0:T(8,128)(2,1)S(1)}, bf16[128,1024]{1,0:T(8,128)(2,1)}, u32[]{:S(2)}) copy-start(bf16[128,1024]{1,0:T(8,128)(2,1)} %key.1) | copy-start | bytes 786436
  3.3 0.9 %copy-start.2 = (bf16[128,1024]{1,0:T(8,128)(2,1)S(1)}, bf16[128,1024]{1,0:T(8,128)(2,1)}, u32[]{:S(2)}) copy-start(bf16[128,1024]{1,0:T(8,128)(2,1)} %value.1) | copy-start | bytes 786436
  4.2 0.9 %copy-start.3 = (bf16[128,1024]{1,0:T(8,128)(2,1)S(1)}, bf16[128,1024]{1,0:T(8,128)(2,1)}, u32[]{:S(2)}) copy-start(bf16[128,1024]{1,0:T(8,128)(2,1)} %grad_out.1) | copy-start | bytes 786436
  36.8 0.7 copy-start.4
where the time goes:
time: 80.3 us
  Pallas kernels  74.4 us (93%)
  local copies, waits for them, and re-layouts  5.21 us (6%)
    pallas_call x1, Pallas kernels, on_device_whole(): pl.pallas_call(functools.partial(spread_kernel, pairs), out_shape=(own_pi...  31.6 us
    pallas_call x1, Pallas kernels, on_device_whole(): pl.pallas_call(functools.partial(collect_kernel, pairs), out_shape=(own_p...  28 us
    pallas_call x1, Pallas kernels, on_device_whole(): pl.pallas_call(functools.partial(attend_kernel, blocks), out_shape=(own_p...  13.7 us
    unnamed x11, local copies, waits for them, and re-layouts  5.21 us

commit v1 on v0

--- a/solution.py
+++ b/solution.py
@@ -198,6 +198,10 @@
 VMEM_BYTES = 20 * 1024 * 1024
 
 
+def left_in_hbm(array):
+    return pltpu.with_memory_space_constraint(array, pltpu.HBM)
+
+
 def place_of():
     index = lax.axis_index("ctx") * lax.axis_size("head") + lax.axis_index("head")
     return lax.div(index, 2), lax.rem(index, 2)
@@ -336,7 +340,8 @@
 
 
 def attend_kernel(
-    blocks, neighbour_hbm, counts, qd, kv, kvt, od, totals, neighbour, pair_scr, x_scr, load
+    blocks, neighbour_hbm, counts_hbm, qd, kv, kvt, od, totals,
+    neighbour, counts, pair_scr, x_scr, load
 ):
     _, side = place_of()
     half = blocks // 2
@@ -344,8 +349,10 @@
     exp_scale = scale * math.log2(math.e)
     low = lax.broadcasted_iota(jnp.int32, (BLK, 2 * E), 1) < E
     top = lax.broadcasted_iota(jnp.int32, (2 * E, BLK), 0) < E
-    names_copy = pltpu.make_async_copy(neighbour_hbm, neighbour, load)
+    names_copy = pltpu.make_async_copy(neighbour_hbm, neighbour, load.at[0])
     names_copy.start()
+    counts_copy = pltpu.make_async_copy(counts_hbm, counts, load.at[1])
+    counts_copy.start()
 
     def clear(block, carry):
         totals[block] = jnp.zeros((BLK, 2 * E), F32)
@@ -353,6 +360,7 @@
 
     lax.fori_loop(0, blocks, clear, 0)
     names_copy.wait()
+    counts_copy.wait()
 
     def folded(array, op):
         return op(array.reshape(BLK // 8, 8, BLK), axis=0)
@@ -361,7 +369,7 @@
         both = qd[place]
         zero = jnp.zeros_like(both)
         spread = jnp.concatenate([jnp.where(low, both, zero), jnp.where(low, zero, both)], axis=0)
-        names = [neighbour[block, slot] for slot in range(used)]
+        names = [neighbour[slot, block] for slot in range(used)]
         highest = None
         for slot in range(used):
             result = lax.dot_general(
@@ -507,7 +515,6 @@
     blocks = 2 * pairs
     width = query.shape[1]
     in_vmem = pl.BlockSpec(memory_space=pltpu.VMEM)
-    in_smem = pl.BlockSpec(memory_space=pltpu.SMEM)
     in_hbm = pl.BlockSpec(memory_space=pltpu.HBM)
     many = pltpu.SemaphoreType.DMA((pairs,))
     piece = (BLK, 2 * E)
@@ -516,7 +523,7 @@
     with jax.named_scope("spread_heads"):
         qd, kv, kvt = pl.pallas_call(
             functools.partial(spread_kernel, pairs),
-            out_shape=(own_pieces, all_pieces, all_pieces),
+            out_shape=tuple(pltpu.VMEM((count, *piece), BF16) for count in (pairs, blocks, blocks)),
             in_specs=[in_hbm] * 4,
             out_specs=(in_vmem,) * 3,
             scratch_shapes=[pltpu.VMEM((4, BLK, width), BF16)]
@@ -526,21 +533,22 @@
             compiler_params=pltpu.CompilerParams(
                 collective_id=0, has_side_effects=True, vmem_limit_bytes=VMEM_BYTES
             ),
-        )(query, key, value, grad_out)
+        )(*map(left_in_hbm, (query, key, value, grad_out)))
     with jax.named_scope("block_attention"):
         od, totals = pl.pallas_call(
             functools.partial(attend_kernel, blocks),
             out_shape=(own_pieces, jax.ShapeDtypeStruct((blocks, *piece), F32)),
-            in_specs=[in_hbm, in_smem] + [in_vmem] * 3,
+            in_specs=[in_hbm] * 2 + [in_vmem] * 3,
             out_specs=(in_vmem,) * 2,
             scratch_shapes=[
-                pltpu.SMEM(neighbour.shape, jnp.int32),
+                pltpu.SMEM(neighbour.shape[::-1], jnp.int32),
+                pltpu.SMEM(counts.shape, jnp.int32),
                 pltpu.VMEM((NNB, BLK, 2 * BLK), F32),
                 pltpu.VMEM((NNB, BLK, 2 * BLK), BF16),
-                pltpu.SemaphoreType.DMA(()),
+                pltpu.SemaphoreType.DMA((2,)),
             ],
             compiler_params=pltpu.CompilerParams(vmem_limit_bytes=VMEM_BYTES),
-        )(neighbour, counts, qd, kv, kvt)
+        )(left_in_hbm(neighbour.T), left_in_hbm(counts), qd, kv, kvt)
     with jax.named_scope("collect_heads"):
         got_od, got_kv = pl.pallas_call(
             functools.partial(collect_kernel, pairs),

time: 80.3 us -> 74.7 us (0.930)
  local copies, waits for them, and re-layouts: 5.21 us -> 0 us
    unnamed x11 -> x0, local copies, waits for them, and re-layouts: 5.21 us -> none
    pallas_call x1, Pallas kernels: 13.7 us -> 12.5 us  [on_device_whole(): pl.pallas_call(functools.partial(attend_kernel, blocks), out_shape=(own_p...]
    pallas_call x1, Pallas kernels: 28 us -> 28.9 us  [on_device_whole(): pl.pallas_call(functools.partial(collect_kernel, pairs), out_shape=(own_p...]
where the time goes in v1:
time: 74.7 us; the launch traced here: 74.8 us
  Pallas kernels  74.1 us (99%)
    pallas_call x1, Pallas kernels, on_device_whole(): pl.pallas_call(functools.partial(spread_kernel, pairs), out_shape=tuple((...  31.5 us
    pallas_call x1, Pallas kernels, on_device_whole(): pl.pallas_call(functools.partial(collect_kernel, pairs), out_shape=(own_p...  28.9 us
    pallas_call x1, Pallas kernels, on_device_whole(): pl.pallas_call(functools.partial(attend_kernel, blocks), out_shape=(own_p...  12.5 us

profile of v1, /device:TPU:0, one launch (start us, length us, event | category | flops | bytes accessed | tf_op | source)
XLA Modules:
  0.0 74.8 jit_solution(12605238512752207913)
XLA Ops:
  0.6 31.5 %spread_heads.1 = (bf16[16,128,128]{2,1,0:T(8,128)(2,1)S(1)}, bf16[32,128,128]{2,1,0:T(8,128)(2,1)S(1)}, bf16[32,128,128]{2,1,0:T(8,128)(2,1)S(1)}) custom-call(bf16[128,1024]{1,0:T(8,128)(2,1)} %query.1, bf16[128,1024]{1,0:T(8,128)(2,1)} %key.1, bf16[128,1024]{1,0:T(8,128)(2,1)} %value.1, bf16[128,1024]{1,0:T(8,128)(2,1)} %grad_out.1), custom_call_target="tpu_custom_call" | custom-call | tf_op jit(solution)/shard_map/spread_heads/pallas_call | solution.py:524
  32.2 12.5 %block_attention.1 = (bf16[16,128,128]{2,1,0:T(8,128)(2,1)S(1)}, f32[32,128,128]{2,1,0:T(8,128)S(1)}) custom-call(s32[8,32]{1,0:T(8,128)} %bitcast.1, s32[32]{0:T(128)} %counts_hbm.1, bf16[16,128,128]{2,1,0:T(8,128)(2,1)S(1)} %get-tuple-element.11.qd, bf16[32,128,128]{2,1,0:T(8,128)(2,1)S(1)} %get-tuple-element.12.kv, ...), custom_call_target="tpu_custom_call" | custom-call | tf_op jit(solution)/shard_map/block_attention/pallas_call | solution.py:538
  44.7 28.9 %collect_heads.1 = (bf16[16,128,128]{2,1,0:T(8,128)(2,1)S(1)}, bf16[16,128,128]{2,1,0:T(8,128)(2,1)S(1)}) custom-call(bf16[16,128,128]{2,1,0:T(8,128)(2,1)S(1)} %get-tuple-element.14.od, f32[32,128,128]{2,1,0:T(8,128)S(1)} %get-tuple-element.15.totals), custom_call_target="tpu_custom_call" | custom-call | tf_op jit(solution)/shard_map/collect_heads/pallas_call | solution.py:553
  73.6 1.1 %join_heads.1 = (bf16[128,1024]{1,0:T(8,128)(2,1)}, bf16[128,1024]{1,0:T(8,128)(2,1)}, bf16[128,1024]{1,0:T(8,128)(2,1)}, bf16[128,1024]{1,0:T(8,128)(2,1)}) custom-call(bf16[16,128,128]{2,1,0:T(8,128)(2,1)S(1)} %get-tuple-element.16.got_od, bf16[16,128,128]{2,1,0:T(8,128)(2,1)S(1)} %get-tuple-element.17.got_kv), custom_call_target="tpu_custom_call" | custom-call | tf_op jit(solution)/shard_map/join_heads/pallas_call | solution.py:564

commit v2 on v1

--- a/solution.py
+++ b/solution.py
@@ -195,6 +195,7 @@
 MESH_ID = pl.DeviceIdType.MESH
 F32 = jnp.float32
 BF16 = jnp.bfloat16
+GROUP = 2
 VMEM_BYTES = 20 * 1024 * 1024
 
 
@@ -341,7 +342,7 @@
 
 def attend_kernel(
     blocks, neighbour_hbm, counts_hbm, qd, kv, kvt, od, totals,
-    neighbour, counts, pair_scr, x_scr, load
+    neighbour, counts, starts, order, pair_scr, x_scr, load
 ):
     _, side = place_of()
     half = blocks // 2
@@ -365,56 +366,95 @@
     def folded(array, op):
         return op(array.reshape(BLK // 8, 8, BLK), axis=0)
 
-    def rows_with(place, block, used):
-        both = qd[place]
-        zero = jnp.zeros_like(both)
-        spread = jnp.concatenate([jnp.where(low, both, zero), jnp.where(low, zero, both)], axis=0)
-        names = [neighbour[slot, block] for slot in range(used)]
-        highest = None
+    def sort_by_used():
+        for used in range(NNB + 1):
+            starts[used] = 0
+        for place in range(half):
+            used = counts[2 * place + side]
+            starts[used - 1] = starts[used - 1] + 1
+        for used in range(NNB - 1, -1, -1):
+            starts[used] = starts[used] + starts[used + 1]
+        for place in range(half):
+            used = counts[2 * place + side]
+            at = starts[used]
+            order[at] = place
+            starts[used] = at + 1
+
+    def rows_with(places, used):
+        group = range(len(places))
+        blocks_now = [2 * place + side for place in places]
+        names = [[neighbour[slot, block] for slot in range(used)] for block in blocks_now]
+        valid = [[slot < counts[block] for slot in range(used)] for block in blocks_now]
+        spread, ahead = [], []
+        for place in places:
+            both = qd[place]
+            zero = jnp.zeros_like(both)
+            upper = jnp.where(low, both, zero)
+            lower = jnp.where(low, zero, both)
+            spread.append(jnp.concatenate([upper, lower], axis=0))
+            ahead.append(jnp.concatenate([upper, lower * jnp.asarray(scale, BF16)], axis=0))
+        highest = [None for _ in group]
         for slot in range(used):
-            result = lax.dot_general(
-                kv[names[slot]], spread, (((1,), (1,)), ((), ())), preferred_element_type=F32
-            )
-            pair_scr[slot] = result
-            part = folded(result[:, :BLK], jnp.max)
-            highest = part if highest is None else jnp.maximum(highest, part)
-        highest = jnp.max(highest, axis=0, keepdims=True)
-        total = jnp.zeros((8, BLK), F32)
-        delta = jnp.zeros((8, BLK), F32)
+            for one in group:
+                result = lax.dot_general(
+                    kv[names[one][slot]],
+                    ahead[one],
+                    (((1,), (1,)), ((), ())),
+                    preferred_element_type=F32,
+                )
+                pair_scr[one, slot] = result
+                part = folded(result[:, :BLK], jnp.max)
+                if one > 0 and slot > 0:
+                    part = jnp.where(valid[one][slot], part, -jnp.inf)
+                highest[one] = part if slot == 0 else jnp.maximum(highest[one], part)
+        highest = [jnp.max(part, axis=0, keepdims=True) for part in highest]
+        total = [jnp.zeros((8, BLK), F32) for _ in group]
+        delta = [jnp.zeros((8, BLK), F32) for _ in group]
         for slot in range(used):
-            raised = jnp.exp2((pair_scr[slot, :, :BLK] - highest) * exp_scale)
-            pair_scr[slot, :, :BLK] = raised
-            total = total + folded(raised, jnp.sum)
-            delta = delta + folded(raised * pair_scr[slot, :, BLK:], jnp.sum)
-        inverse = 1.0 / jnp.sum(total, axis=0, keepdims=True)
-        delta = jnp.sum(delta, axis=0, keepdims=True) * inverse
+            for one in group:
+                raised = jnp.exp2((pair_scr[one, slot, :, :BLK] - highest[one]) * exp_scale)
+                if one > 0 and slot > 0:
+                    raised = jnp.where(valid[one][slot], raised, 0.0)
+                pair_scr[one, slot, :, :BLK] = raised
+                total[one] = total[one] + folded(raised, jnp.sum)
+                delta[one] = delta[one] + folded(raised * pair_scr[one, slot, :, BLK:], jnp.sum)
+        inverse = [1.0 / jnp.sum(part, axis=0, keepdims=True) for part in total]
+        delta = [jnp.sum(delta[one], axis=0, keepdims=True) * inverse[one] for one in group]
         for slot in range(used):
-            probability = pair_scr[slot, :, :BLK] * inverse
-            dscore = (probability * scale) * (pair_scr[slot, :, BLK:] - delta)
-            x_scr[slot] = jnp.concatenate(
-                [dscore.astype(BF16), probability.astype(BF16)], axis=1
-            )
-        rows = jnp.zeros((2 * E, 2 * BLK), F32)
-        for slot in range(0, used, 2):
-            if slot + 1 < used:
-                keys_t = jnp.concatenate([kvt[names[slot]], kvt[names[slot + 1]]], axis=1)
-                grads = jnp.concatenate([x_scr[slot], x_scr[slot + 1]], axis=0)
-            else:
-                keys_t = kvt[names[slot]]
-                grads = x_scr[slot]
-            rows = rows + jnp.dot(keys_t, grads, preferred_element_type=F32)
+            for one in group:
+                probability = pair_scr[one, slot, :, :BLK] * inverse[one]
+                dscore = probability * (pair_scr[one, slot, :, BLK:] - delta[one])
+                x_scr[one, slot] = jnp.concatenate(
+                    [dscore.astype(BF16), probability.astype(BF16)], axis=1
+                )
+        for one in group:
+            rows = jnp.zeros((2 * E, 2 * BLK), F32)
+            for slot in range(0, used, 2):
+                if slot + 1 < used:
+                    keys_t = jnp.concatenate(
+                        [kvt[names[one][slot]], kvt[names[one][slot + 1]]], axis=1
+                    )
+                    grads = jnp.concatenate([x_scr[one, slot], x_scr[one, slot + 1]], axis=0)
+                else:
+                    keys_t = kvt[names[one][slot]]
+                    grads = x_scr[one, slot]
+                rows = rows + jnp.dot(keys_t, grads, preferred_element_type=F32)
+            od[places[one]] = jnp.where(top, rows[:, :BLK], rows[:, BLK:]).T.astype(BF16)
         for slot in range(used):
-            totals[names[slot]] += jnp.dot(x_scr[slot], spread, preferred_element_type=F32)
-        od[place] = jnp.where(top, rows[:, :BLK], rows[:, BLK:]).T.astype(BF16)
-
-    def one_block(place, carry):
-        block = 2 * place + side
-        used_now = counts[block]
+            for one in group:
+                totals[names[one][slot]] += jnp.dot(
+                    x_scr[one, slot], spread[one], preferred_element_type=F32
+                )
+
+    def one_group(turn, carry):
+        places = [order[GROUP * turn + one] for one in range(GROUP)]
+        used_now = counts[2 * places[0] + side]
         for used in range(1, NNB + 1):
-            pl.when(used_now == used)(functools.partial(rows_with, place, block, used))
+            pl.when(used_now == used)(functools.partial(rows_with, places, used))
         return carry
 
-    lax.fori_loop(0, half, one_block, 0)
+    sort_by_used()
+    lax.fori_loop(0, half // GROUP, one_group, 0)
 
 
 def collect_kernel(
@@ -543,8 +583,10 @@
             scratch_shapes=[
                 pltpu.SMEM(neighbour.shape[::-1], jnp.int32),
                 pltpu.SMEM(counts.shape, jnp.int32),
-                pltpu.VMEM((NNB, BLK, 2 * BLK), F32),
-                pltpu.VMEM((NNB, BLK, 2 * BLK), BF16),
+                pltpu.SMEM((NNB + 1,), jnp.int32),
+                pltpu.SMEM((pairs,), jnp.int32),
+                pltpu.VMEM((GROUP, NNB, BLK, 2 * BLK), F32),
+                pltpu.VMEM((GROUP, NNB, BLK, 2 * BLK), BF16),
                 pltpu.SemaphoreType.DMA((2,)),
             ],
             compiler_params=pltpu.CompilerParams(vmem_limit_bytes=VMEM_BYTES),
@@ -576,7 +618,7 @@
 
 def on_device(query, key, value, grad_out, neighbour, counts):
     devices = lax.axis_size("ctx") * lax.axis_size("head")
-    if devices == 2 * H and query.shape == (BLK, H * E) and counts.shape[0] == devices:
+    if devices == 2 * H and H % GROUP == 0 and query.shape == (BLK, H * E) and counts.shape[0] == devices:
         return on_device_whole(query, key, value, grad_out, neighbour, counts)
     return on_device_windowed(query, key, value, grad_out, neighbour, counts)
 

time: 74.7 us -> 72 us (0.964)
  Pallas kernels: 74.1 us -> 71.6 us
    pallas_call x1, Pallas kernels: 28.9 us -> 27.6 us  [on_device_whole(): pl.pallas_call(functools.partial(collect_kernel, pairs), out_shape=(own_p...]
    pallas_call x1, Pallas kernels: 12.5 us -> 11.3 us  [on_device_whole(): pl.pallas_call(functools.partial(attend_kernel, blocks), out_shape=(own_p...]
where the time goes in v2:
time: 72 us; the launch traced here: 72.2 us
  Pallas kernels  71.6 us (99%)
    pallas_call x1, Pallas kernels, on_device_whole(): pl.pallas_call(functools.partial(spread_kernel, pairs), out_shape=tuple((...  31.5 us
    pallas_call x1, Pallas kernels, on_device_whole(): pl.pallas_call(functools.partial(collect_kernel, pairs), out_shape=(own_p...  27.6 us
    pallas_call x1, Pallas kernels, on_device_whole(): pl.pallas_call(functools.partial(attend_kernel, blocks), out_shape=(own_p...  11.3 us

profile of v2, /device:TPU:0, one launch (start us, length us, event | category | flops | bytes accessed | tf_op | source)
XLA Modules:
  0.0 72.2 jit_solution(844186473276971068)
XLA Ops:
  0.6 31.5 %spread_heads.1 = (bf16[16,128,128]{2,1,0:T(8,128)(2,1)S(1)}, bf16[32,128,128]{2,1,0:T(8,128)(2,1)S(1)}, bf16[32,128,128]{2,1,0:T(8,128)(2,1)S(1)}) custom-call(bf16[128,1024]{1,0:T(8,128)(2,1)} %query.1, bf16[128,1024]{1,0:T(8,128)(2,1)} %key.1, bf16[128,1024]{1,0:T(8,128)(2,1)} %value.1, bf16[128,1024]{1,0:T(8,128)(2,1)} %grad_out.1), custom_call_target="tpu_custom_call" | custom-call | tf_op jit(solution)/shard_map/spread_heads/pallas_call | solution.py:564
  32.2 11.3 %block_attention.1 = (bf16[16,128,128]{2,1,0:T(8,128)(2,1)S(1)}, f32[32,128,128]{2,1,0:T(8,128)S(1)}) custom-call(s32[8,32]{1,0:T(8,128)} %bitcast.1, s32[32]{0:T(128)} %counts_hbm.1, bf16[16,128,128]{2,1,0:T(8,128)(2,1)S(1)} %get-tuple-element.11.qd, bf16[32,128,128]{2,1,0:T(8,128)(2,1)S(1)} %get-tuple-element.12.kv, ...), custom_call_target="tpu_custom_call" | custom-call | tf_op jit(solution)/shard_map/block_attention/pallas_call | solution.py:578
  43.5 27.6 %collect_heads.1 = (bf16[16,128,128]{2,1,0:T(8,128)(2,1)S(1)}, bf16[16,128,128]{2,1,0:T(8,128)(2,1)S(1)}) custom-call(bf16[16,128,128]{2,1,0:T(8,128)(2,1)S(1)} %get-tuple-element.14.od, f32[32,128,128]{2,1,0:T(8,128)S(1)} %get-tuple-element.15.totals), custom_call_target="tpu_custom_call" | custom-call | tf_op jit(solution)/shard_map/collect_heads/pallas_call | solution.py:595
  71.1 1.1 %join_heads.1 = (bf16[128,1024]{1,0:T(8,128)(2,1)}, bf16[128,1024]{1,0:T(8,128)(2,1)}, bf16[128,1024]{1,0:T(8,128)(2,1)}, bf16[128,1024]{1,0:T(8,128)(2,1)}) custom-call(bf16[16,128,128]{2,1,0:T(8,128)(2,1)S(1)} %get-tuple-element.16.got_od, bf16[16,128,128]{2,1,0:T(8,128)(2,1)S(1)} %get-tuple-element.17.got_kv), custom_call_target="tpu_custom_call" | custom-call | tf_op jit(solution)/shard_map/join_heads/pallas_call | solution.py:606

commit v3 on v2

--- a/solution.py
+++ b/solution.py
@@ -195,7 +195,7 @@
 MESH_ID = pl.DeviceIdType.MESH
 F32 = jnp.float32
 BF16 = jnp.bfloat16
-GROUP = 2
+GROUP = 4
 VMEM_BYTES = 20 * 1024 * 1024
 
 

time: 72 us -> 70.7 us (0.982)
  Pallas kernels: 71.6 us -> 70.2 us
    pallas_call x1, Pallas kernels: 11.3 us -> 9.8 us  [on_device_whole(): pl.pallas_call(functools.partial(attend_kernel, blocks), out_shape=(own_p...]
where the time goes in v3:
time: 70.7 us; the launch traced here: 70.9 us
  Pallas kernels  70.2 us (99%)
    pallas_call x1, Pallas kernels, on_device_whole(): pl.pallas_call(functools.partial(spread_kernel, pairs), out_shape=tuple((...  31.5 us
    pallas_call x1, Pallas kernels, on_device_whole(): pl.pallas_call(functools.partial(collect_kernel, pairs), out_shape=(own_p...  27.7 us
    pallas_call x1, Pallas kernels, on_device_whole(): pl.pallas_call(functools.partial(attend_kernel, blocks), out_shape=(own_p...  9.8 us

profile of v3, /device:TPU:0, one launch (start us, length us, event | category | flops | bytes accessed | tf_op | source)
XLA Modules:
  0.0 70.9 jit_solution(315410384233994110)
XLA Ops:
  0.6 31.5 %spread_heads.1 = (bf16[16,128,128]{2,1,0:T(8,128)(2,1)S(1)}, bf16[32,128,128]{2,1,0:T(8,128)(2,1)S(1)}, bf16[32,128,128]{2,1,0:T(8,128)(2,1)S(1)}) custom-call(bf16[128,1024]{1,0:T(8,128)(2,1)} %query.1, bf16[128,1024]{1,0:T(8,128)(2,1)} %key.1, bf16[128,1024]{1,0:T(8,128)(2,1)} %value.1, bf16[128,1024]{1,0:T(8,128)(2,1)} %grad_out.1), custom_call_target="tpu_custom_call" | custom-call | tf_op jit(solution)/shard_map/spread_heads/pallas_call | solution.py:564
  32.2 9.8 %block_attention.1 = (bf16[16,128,128]{2,1,0:T(8,128)(2,1)S(1)}, f32[32,128,128]{2,1,0:T(8,128)S(1)}) custom-call(s32[8,32]{1,0:T(8,128)} %bitcast.1, s32[32]{0:T(128)} %counts_hbm.1, bf16[16,128,128]{2,1,0:T(8,128)(2,1)S(1)} %get-tuple-element.11.qd, bf16[32,128,128]{2,1,0:T(8,128)(2,1)S(1)} %get-tuple-element.12.kv, ...), custom_call_target="tpu_custom_call" | custom-call | tf_op jit(solution)/shard_map/block_attention/pallas_call | solution.py:578
  42.0 27.7 %collect_heads.1 = (bf16[16,128,128]{2,1,0:T(8,128)(2,1)S(1)}, bf16[16,128,128]{2,1,0:T(8,128)(2,1)S(1)}) custom-call(bf16[16,128,128]{2,1,0:T(8,128)(2,1)S(1)} %get-tuple-element.14.od, f32[32,128,128]{2,1,0:T(8,128)S(1)} %get-tuple-element.15.totals), custom_call_target="tpu_custom_call" | custom-call | tf_op jit(solution)/shard_map/collect_heads/pallas_call | solution.py:595
  69.7 1.1 %join_heads.1 = (bf16[128,1024]{1,0:T(8,128)(2,1)}, bf16[128,1024]{1,0:T(8,128)(2,1)}, bf16[128,1024]{1,0:T(8,128)(2,1)}, bf16[128,1024]{1,0:T(8,128)(2,1)}) custom-call(bf16[16,128,128]{2,1,0:T(8,128)(2,1)S(1)} %get-tuple-element.16.got_od, bf16[16,128,128]{2,1,0:T(8,128)(2,1)S(1)} %get-tuple-element.17.got_kv), custom_call_target="tpu_custom_call" | custom-call | tf_op jit(solution)/shard_map/join_heads/pallas_call | solution.py:606

commit v4 on v2

--- a/solution.py
+++ b/solution.py
@@ -394,16 +394,359 @@
             spread.append(jnp.concatenate([upper, lower], axis=0))
             ahead.append(jnp.concatenate([upper, lower * jnp.asarray(scale, BF16)], axis=0))
         highest = [None for _ in group]
+        for one in group:
+            keys = jnp.concatenate([kv[name] for name in names[one]], axis=0)
+            result = lax.dot_general(
+                keys, ahead[one], (((1,), (1,)), ((), ())), preferred_element_type=F32
+            ).reshape(used, BLK, 2 * BLK)
+            for slot in range(used):
+                pair_scr[one, slot] = result[slot]
+                part = folded(result[slot, :, :BLK], jnp.max)
+                if one > 0 and slot > 0:
+                    part = jnp.where(valid[one][slot], part, -jnp.inf)
+                highest[one] = part if slot == 0 else jnp.maximum(highest[one], part)
+        highest = [jnp.max(part, axis=0, keepdims=True) for part in highest]
+        total = [jnp.zeros((8, BLK), F32) for _ in group]
+        delta = [jnp.zeros((8, BLK), F32) for _ in group]
         for slot in range(used):
             for one in group:
-                result = lax.dot_general(
-                    kv[names[one][slot]],
-                    ahead[one],
-                    (((1,), (1,)), ((), ())),
-                    preferred_element_type=F32,
+                raised = jnp.exp2((pair_scr[one, slot, :, :BLK] - highest[one]) * exp_scale)
+                if one > 0 and slot > 0:
+                    raised = jnp.where(valid[one][slot], raised, 0.0)
+                pair_scr[one, slot, :, :BLK] = raised
+                total[one] = total[one] + folded(raised, jnp.sum)
+                delta[one] = delta[one] + folded(raised * pair_scr[one, slot, :, BLK:], jnp.sum)
+        inverse = [1.0 / jnp.sum(part, axis=0, keepdims=True) for part in total]
+        delta = [jnp.sum(delta[one], axis=0, keepdims=True) * inverse[one] for one in group]
+        for slot in range(used):
+            for one in group:
+                probability = pair_scr[one, slot, :, :BLK] * inverse[one]
+                dscore = probability * (pair_scr[one, slot, :, BLK:] - delta[one])
+                x_scr[one, slot] = jnp.concatenate(
+                    [dscore.astype(BF16), probability.astype(BF16)], axis=1
                 )
-                pair_scr[one, slot] = result
-                part = folded(result[:, :BLK], jnp.max)
+        for one in group:
+            rows = jnp.zeros((2 * E, 2 * BLK), F32)
+            for slot in range(0, used, 2):
+                if slot + 1 < used:
+                    keys_t = jnp.concatenate(
+                        [kvt[names[one][slot]], kvt[names[one][slot + 1]]], axis=1
+                    )
+                    grads = jnp.concatenate([x_scr[one, slot], x_scr[one, slot + 1]], axis=0)
+                else:
+                    keys_t = kvt[names[one][slot]]
+                    grads = x_scr[one, slot]
+                rows = rows + jnp.dot(keys_t, grads, preferred_element_type=F32)
+            od[places[one]] = jnp.where(top, rows[:, :BLK], rows[:, BLK:]).T.astype(BF16)
+        for one in group:
+            grads = x_scr[one, :used].reshape(used * BLK, 2 * BLK)
+            added = jnp.dot(grads, spread[one], preferred_element_type=F32)
+            for slot in range(used):
+                totals[names[one][slot]] += added[slot * BLK : (slot + 1) * BLK]
+
+    def one_group(totals, inputs):
+        queries, cotangent, chosen, used_now = inputs
+        selected = window[chosen]
+        keys_sel = selected[..., :head_cols].reshape(per_group, NNB, BLK, per_dev, E)
+        values_sel = selected[..., head_cols:].reshape(per_group, NNB, BLK, per_dev, E)
+        usable = jnp.arange(NNB)[None, :] < used_now[:, None]
+        allowed = usable[:, None, None, :, None]
+        scores = (
+            jnp.einsum("rihe,rjthe->rhijt", queries, keys_sel, preferred_element_type=jnp.float32)
+            * scale_factor
+        )
+        masked = jnp.where(allowed, scores, -1e30)
+        highest = jnp.max(masked, axis=(3, 4), keepdims=True)
+        raised = jnp.where(allowed, jnp.exp(masked - highest), 0.0)
+        total = jnp.sum(raised, axis=(3, 4), keepdims=True)
+        probability = raised / total
+        weights = probability.astype(jnp.bfloat16)
+        out_rows = jnp.einsum(
+            "rhijt,rjthe->rihe", weights, values_sel, preferred_element_type=jnp.float32
+        ).astype(jnp.bfloat16)
+        dprob = jnp.einsum(
+            "rihe,rjthe->rhijt", cotangent, values_sel, preferred_element_type=jnp.float32
+        )
+        row_delta = jnp.sum(probability * dprob, axis=(3, 4), keepdims=True)
+        dscore = (probability * (dprob - row_delta) * scale_factor).astype(jnp.bfloat16)
+        dquery = jnp.einsum(
+            "rhijt,rjthe->rihe", dscore, keys_sel, preferred_element_type=jnp.float32
+        ).astype(jnp.bfloat16)
+        dkey_part = jnp.einsum(
+            "rhijt,rihe->rjthe", dscore, queries, preferred_element_type=jnp.float32
+        )
+        dvalue_part = jnp.einsum(
+            "rhijt,rihe->rjthe", weights, cotangent, preferred_element_type=jnp.float32
+        )
+        joined = jnp.concatenate(
+            [
+                dkey_part.reshape(per_group * NNB, BLK, head_cols),
+                dvalue_part.reshape(per_group * NNB, BLK, head_cols),
+            ],
+            axis=-1,
+        )
+        totals = totals.at[chosen.reshape(-1)].add(joined)
+        return (totals, (out_rows, dquery))
+
+    start_grads = jnp.zeros((span_shards * blocks_shard, BLK, 2 * head_cols), jnp.float32)
+    grads_window, results = lax.scan(one_group, start_grads, (query_g, grad_g, index_g, used_g))
+    grads_window = grads_window.reshape(span_shards, shard_rows, 2 * head_cols)
+    combined = grads_window[REACH]
+    offsets_back = list(range(1, REACH + 1)) + [-offset for offset in range(1, REACH + 1)]
+    for offset in offsets_back:
+        combined = combined + passed_along(
+            grads_window[REACH - offset].astype(jnp.bfloat16), "ctx", -offset
+        ).astype(jnp.float32)
+    combined = combined.astype(jnp.bfloat16)
+    dkey_s = combined[:, :head_cols]
+    dvalue_s = combined[:, head_cols:]
+    out_s = results[0].reshape(shard_rows, head_cols)
+    dquery_s = results[1].reshape(shard_rows, head_cols)
+    back = (
+        lax.all_to_all(
+            out_s.reshape(shard_rows, 1, head_cols), "head", split_axis=0, concat_axis=1, tiled=True
+        ),
+        lax.all_to_all(
+            dquery_s.reshape(shard_rows, 1, head_cols),
+            "head",
+            split_axis=0,
+            concat_axis=1,
+            tiled=True,
+        ),
+        lax.all_to_all(
+            dkey_s.reshape(shard_rows, 1, head_cols),
+            "head",
+            split_axis=0,
+            concat_axis=1,
+            tiled=True,
+        ),
+        lax.all_to_all(
+            dvalue_s.reshape(shard_rows, 1, head_cols),
+            "head",
+            split_axis=0,
+            concat_axis=1,
+            tiled=True,
+        ),
+    )
+    width = groups * head_cols
+    return (
+        back[0].reshape(tok_rows, width),
+        back[1].reshape(tok_rows, width),
+        back[2].reshape(tok_rows, width),
+        back[3].reshape(tok_rows, width),
+    )
+
+
+MESH_ID = pl.DeviceIdType.MESH
+F32 = jnp.float32
+BF16 = jnp.bfloat16
+GROUP = 2
+VMEM_BYTES = 20 * 1024 * 1024
+
+
+def left_in_hbm(array):
+    return pltpu.with_memory_space_constraint(array, pltpu.HBM)
+
+
+def place_of():
+    index = lax.axis_index("ctx") * lax.axis_size("head") + lax.axis_index("head")
+    return lax.div(index, 2), lax.rem(index, 2)
+
+
+def device_of(owner, side):
+    n_head = lax.axis_size("head")
+    index = 2 * owner + side
+    return (lax.div(index, n_head), lax.rem(index, n_head))
+
+
+def partners(pairs, owner, step):
+    half = pairs // 2
+    far = 1 - lax.div(step, half)
+    base = lax.rem(lax.div(owner, half) + far, 2) * half
+    low, turn = lax.rem(owner, half), lax.rem(step, half)
+    return base + lax.rem(low + turn, half), base + lax.rem(low - turn + half, half)
+
+
+def each_step(pairs, body):
+    def one(step, carry):
+        body(step)
+        return carry
+
+    lax.fori_loop(0, pairs // 2, one, 0)
+    lax.fori_loop(pairs // 2 + 1, pairs, one, 0)
+
+
+def greet(pairs):
+    owner, side = place_of()
+    barrier = pltpu.get_barrier_semaphore()
+    pl.semaphore_signal(barrier, inc=1, device_id=device_of(owner, 1 - side), device_id_type=MESH_ID)
+
+    def one(step):
+        to, _ = partners(pairs, owner, step)
+        pl.semaphore_signal(barrier, inc=1, device_id=device_of(to, side), device_id_type=MESH_ID)
+
+    each_step(pairs, one)
+    return barrier
+
+
+def spread_kernel(
+    pairs, query, key, value, grad_out, qd, kv, kvt, own_rows, send_qd, send_kv,
+    load, qd_out, qd_in, kv_out, kv_in, share_out, share_in,
+):
+    owner, side = place_of()
+    loads = [
+        pltpu.make_async_copy(array, own_rows.at[place], load.at[place])
+        for place, array in enumerate((key, value, query, grad_out))
+    ]
+    for copy in loads:
+        copy.start()
+    barrier = greet(pairs)
+
+    def pack(first, pieces):
+        loads[first].wait()
+        loads[first + 1].wait()
+        for pair in range(pairs // 2):
+            cols = slice(2 * E * pair, 2 * E * (pair + 1))
+            a = own_rows[first, :, cols]
+            b = own_rows[first + 1, :, cols]
+            pieces[2 * pair] = jnp.concatenate([a[:, :E], b[:, :E]], axis=1)
+            pieces[2 * pair + 1] = jnp.concatenate([a[:, E:], b[:, E:]], axis=1)
+
+    def kv_copy(step, to, source):
+        return pltpu.make_async_remote_copy(
+            src_ref=send_kv.at[to],
+            dst_ref=kv.at[2 * source + side],
+            send_sem=kv_out.at[step],
+            recv_sem=kv_in.at[step],
+            device_id=device_of(to, side),
+            device_id_type=MESH_ID,
+        )
+
+    def qd_copy(step, to, source):
+        return pltpu.make_async_remote_copy(
+            src_ref=send_qd.at[to],
+            dst_ref=qd.at[source],
+            send_sem=qd_out.at[step],
+            recv_sem=qd_in.at[step],
+            device_id=device_of(to, side),
+            device_id_type=MESH_ID,
+        )
+
+    def share_copy(step, source, whose):
+        return pltpu.make_async_remote_copy(
+            src_ref=kv.at[2 * source + side],
+            dst_ref=kv.at[2 * source + whose],
+            send_sem=share_out.at[step],
+            recv_sem=share_in.at[step],
+            device_id=device_of(owner, 1 - side),
+            device_id_type=MESH_ID,
+        )
+
+    def send_keys(step):
+        to, _ = partners(pairs, owner, step)
+        kv_copy(step, to, owner).start()
+
+    def send_queries(step):
+        to, _ = partners(pairs, owner, step)
+        qd_copy(step, to, owner).start()
+
+    pack(0, send_kv)
+    pl.semaphore_wait(barrier, pairs)
+    each_step(pairs, send_keys)
+    pack(2, send_qd)
+    each_step(pairs, send_queries)
+    mine = 2 * owner + side
+    kv[mine] = send_kv[owner]
+    qd[owner] = send_qd[owner]
+    share_copy(pairs // 2, owner, side).start()
+    kvt[mine] = kv[mine].T
+
+    def pass_on(step):
+        _, source = partners(pairs, owner, step)
+        kv_copy(step, owner, source).wait_recv()
+        share_copy(step, source, side).start()
+        kvt[2 * source + side] = kv[2 * source + side].T
+
+    def take_share(step):
+        _, source = partners(pairs, owner, step)
+        share_copy(step, source, side).wait_send()
+        share_copy(step, source, 1 - side).wait_recv()
+        kvt[2 * source + 1 - side] = kv[2 * source + 1 - side].T
+
+    def finish(step):
+        to, source = partners(pairs, owner, step)
+        qd_copy(step, owner, source).wait_recv()
+        qd_copy(step, to, owner).wait_send()
+        kv_copy(step, to, owner).wait_send()
+
+    each_step(pairs, pass_on)
+    take_share(jnp.int32(pairs // 2))
+    each_step(pairs, take_share)
+    each_step(pairs, finish)
+
+
+def attend_kernel(
+    blocks, neighbour_hbm, counts_hbm, qd, kv, kvt, od, totals,
+    neighbour, counts, starts, order, pair_scr, x_scr, load
+):
+    _, side = place_of()
+    half = blocks // 2
+    scale = 1.0 / math.sqrt(E)
+    exp_scale = scale * math.log2(math.e)
+    low = lax.broadcasted_iota(jnp.int32, (BLK, 2 * E), 1) < E
+    top = lax.broadcasted_iota(jnp.int32, (2 * E, BLK), 0) < E
+    names_copy = pltpu.make_async_copy(neighbour_hbm, neighbour, load.at[0])
+    names_copy.start()
+    counts_copy = pltpu.make_async_copy(counts_hbm, counts, load.at[1])
+    counts_copy.start()
+
+    def clear(block, carry):
+        totals[block] = jnp.zeros((BLK, 2 * E), F32)
+        return carry
+
+    lax.fori_loop(0, blocks, clear, 0)
+    names_copy.wait()
+    counts_copy.wait()
+
+    def folded(array, op):
+        return op(array.reshape(BLK // 8, 8, BLK), axis=0)
+
+    def sort_by_used():
+        for used in range(NNB + 1):
+            starts[used] = 0
+        for place in range(half):
+            used = counts[2 * place + side]
+            starts[used - 1] = starts[used - 1] + 1
+        for used in range(NNB - 1, -1, -1):
+            starts[used] = starts[used] + starts[used + 1]
+        for place in range(half):
+            used = counts[2 * place + side]
+            at = starts[used]
+            order[at] = place
+            starts[used] = at + 1
+
+    def rows_with(places, used):
+        group = range(len(places))
+        blocks_now = [2 * place + side for place in places]
+        names = [[neighbour[slot, block] for slot in range(used)] for block in blocks_now]
+        valid = [[slot < counts[block] for slot in range(used)] for block in blocks_now]
+        spread, ahead = [], []
+        for place in places:
+            both = qd[place]
+            zero = jnp.zeros_like(both)
+            upper = jnp.where(low, both, zero)
+            lower = jnp.where(low, zero, both)
+            spread.append(jnp.concatenate([upper, lower], axis=0))
+            ahead.append(jnp.concatenate([upper, lower * jnp.asarray(scale, BF16)], axis=0))
+        highest = [None for _ in group]
+        for one in group:
+            keys = jnp.concatenate([kv[name] for name in names[one]], axis=0)
+            result = lax.dot_general(
+                keys, ahead[one], (((1,), (1,)), ((), ())), preferred_element_type=F32
+            ).reshape(used, BLK, 2 * BLK)
+            for slot in range(used):
+                pair_scr[one, slot] = result[slot]
+                part = folded(result[slot, :, :BLK], jnp.max)
                 if one > 0 and slot > 0:
                     part = jnp.where(valid[one][slot], part, -jnp.inf)
                 highest[one] = part if slot == 0 else jnp.maximum(highest[one], part)

time: 72 us -> 72 us (level)
    pallas_call x1, Pallas kernels: 11.3 us -> 9.48 us  [on_device_whole(): pl.pallas_call(functools.partial(attend_kernel, blocks), out_shape=(own_p...]
    pallas_call x1, Pallas kernels: 27.6 us -> 28.8 us  [on_device_whole(): pl.pallas_call(functools.partial(collect_kernel, pairs), out_shape=(own_p...]
where the time goes in v4:
time: 72 us; the launch traced here: 71.6 us
  Pallas kernels  71 us (99%)
    pallas_call x1, Pallas kernels, on_device_whole(): pl.pallas_call(functools.partial(spread_kernel, pairs), out_shape=tuple((...  31.5 us
    pallas_call x1, Pallas kernels, on_device_whole(): pl.pallas_call(functools.partial(collect_kernel, pairs), out_shape=(own_p...  28.8 us
    pallas_call x1, Pallas kernels, on_device_whole(): pl.pallas_call(functools.partial(attend_kernel, blocks), out_shape=(own_p...  9.48 us

profile of v4, /device:TPU:0, one launch (start us, length us, event | category | flops | bytes accessed | tf_op | source)
XLA Modules:
  0.0 71.6 jit_solution(15978558909900352163)
XLA Ops:
  0.6 31.5 %spread_heads.1 = (bf16[16,128,128]{2,1,0:T(8,128)(2,1)S(1)}, bf16[32,128,128]{2,1,0:T(8,128)(2,1)S(1)}, bf16[32,128,128]{2,1,0:T(8,128)(2,1)S(1)}) custom-call(bf16[128,1024]{1,0:T(8,128)(2,1)} %query.1, bf16[128,1024]{1,0:T(8,128)(2,1)} %key.1, bf16[128,1024]{1,0:T(8,128)(2,1)} %value.1, bf16[128,1024]{1,0:T(8,128)(2,1)} %grad_out.1), custom_call_target="tpu_custom_call" | custom-call | tf_op jit(solution)/shard_map/spread_heads/pallas_call | solution.py:907
  32.2 9.5 %block_attention.1 = (bf16[16,128,128]{2,1,0:T(8,128)(2,1)S(1)}, f32[32,128,128]{2,1,0:T(8,128)S(1)}) custom-call(s32[8,32]{1,0:T(8,128)} %bitcast.1, s32[32]{0:T(128)} %counts_hbm.1, bf16[16,128,128]{2,1,0:T(8,128)(2,1)S(1)} %get-tuple-element.11.qd, bf16[32,128,128]{2,1,0:T(8,128)(2,1)S(1)} %get-tuple-element.12.kv, ...), custom_call_target="tpu_custom_call" | custom-call | tf_op jit(solution)/shard_map/block_attention/pallas_call | solution.py:921
  41.6 28.8 %collect_heads.1 = (bf16[16,128,128]{2,1,0:T(8,128)(2,1)S(1)}, bf16[16,128,128]{2,1,0:T(8,128)(2,1)S(1)}) custom-call(bf16[16,128,128]{2,1,0:T(8,128)(2,1)S(1)} %get-tuple-element.14.od, f32[32,128,128]{2,1,0:T(8,128)S(1)} %get-tuple-element.15.totals), custom_call_target="tpu_custom_call" | custom-call | tf_op jit(solution)/shard_map/collect_heads/pallas_call | solution.py:938
  70.5 1.1 %join_heads.1 = (bf16[128,1024]{1,0:T(8,128)(2,1)}, bf16[128,1024]{1,0:T(8,128)(2,1)}, bf16[128,1024]{1,0:T(8,128)(2,1)}, bf16[128,1024]{1,0:T(8,128)(2,1)}) custom-call(bf16[16,128,128]{2,1,0:T(8,128)(2,1)S(1)} %get-tuple-element.16.got_od, bf16[16,128,128]{2,1,0:T(8,128)(2,1)S(1)} %get-tuple-element.17.got_kv), custom_call_target="tpu_custom_call" | custom-call | tf_op jit(solution)/shard_map/join_heads/pallas_call | solution.py:949

commit v5 on v2

--- a/solution.py
+++ b/solution.py
@@ -222,13 +222,25 @@
     return base + lax.rem(low + turn, half), base + lax.rem(low - turn + half, half)
 
 
-def each_step(pairs, body):
+def run_steps(start, stop, body):
     def one(step, carry):
         body(step)
         return carry
 
-    lax.fori_loop(0, pairs // 2, one, 0)
-    lax.fori_loop(pairs // 2 + 1, pairs, one, 0)
+    lax.fori_loop(start, stop, one, 0)
+
+
+def far_steps(pairs, body):
+    run_steps(0, pairs // 2, body)
+
+
+def near_steps(pairs, body):
+    run_steps(pairs // 2 + 1, pairs, body)
+
+
+def each_step(pairs, body):
+    far_steps(pairs, body)
+    near_steps(pairs, body)
 
 
 def greet(pairs):
@@ -245,15 +257,20 @@
 
 
 def spread_kernel(
-    pairs, query, key, value, grad_out, qd, kv, kvt, own_rows, send_qd, send_kv,
+    pairs, query, key, value, grad_out, neighbour_hbm, counts_hbm, qd, kv, kvt, x_near, od_near,
+    own_rows, send_qd, send_kv, neighbour, counts, pair_scr,
     load, qd_out, qd_in, kv_out, kv_in, share_out, share_in,
 ):
     owner, side = place_of()
+    half = pairs // 2
+    near = lax.div(owner, half) * half
     loads = [
         pltpu.make_async_copy(array, own_rows.at[place], load.at[place])
         for place, array in enumerate((key, value, query, grad_out))
     ]
-    for copy in loads:
+    names_copy = pltpu.make_async_copy(neighbour_hbm, neighbour, load.at[4])
+    counts_copy = pltpu.make_async_copy(counts_hbm, counts, load.at[5])
+    for copy in loads + [names_copy, counts_copy]:
         copy.start()
     barrier = greet(pairs)
 
@@ -309,11 +326,11 @@
     pl.semaphore_wait(barrier, pairs)
     each_step(pairs, send_keys)
     pack(2, send_qd)
-    each_step(pairs, send_queries)
+    near_steps(pairs, send_queries)
     mine = 2 * owner + side
     kv[mine] = send_kv[owner]
     qd[owner] = send_qd[owner]
-    share_copy(pairs // 2, owner, side).start()
+    share_copy(half, owner, side).start()
     kvt[mine] = kv[mine].T
 
     def pass_on(step):
@@ -322,34 +339,131 @@
         share_copy(step, source, side).start()
         kvt[2 * source + side] = kv[2 * source + side].T
 
+    def pass_on_far(step):
+        pass_on(step)
+        to, _ = partners(pairs, owner, step)
+        kv_copy(step, to, owner).wait_send()
+        send_queries(step)
+
     def take_share(step):
         _, source = partners(pairs, owner, step)
         share_copy(step, source, side).wait_send()
         share_copy(step, source, 1 - side).wait_recv()
         kvt[2 * source + 1 - side] = kv[2 * source + 1 - side].T
 
-    def finish(step):
+    def take_near(step):
         to, source = partners(pairs, owner, step)
         qd_copy(step, owner, source).wait_recv()
         qd_copy(step, to, owner).wait_send()
         kv_copy(step, to, owner).wait_send()
 
-    each_step(pairs, pass_on)
-    take_share(jnp.int32(pairs // 2))
+    def take_far(step):
+        to, source = partners(pairs, owner, step)
+        qd_copy(step, owner, source).wait_recv()
+        qd_copy(step, to, owner).wait_send()
+
+    def near_group(turn, carry):
+        group = range(GROUP)
+        places = [GROUP * turn + one for one in group]
+        blocks_now = [2 * (near + place) + side for place in places]
+        names = [[neighbour[slot, block] for slot in range(NNB)] for block in blocks_now]
+        valid = [
+            [slot < counts[block] if slot > 0 else None for slot in range(NNB)]
+            for block in blocks_now
+        ]
+        queries = [qd[near + place] for place in places]
+        x_out = [x_near.at[place] for place in places]
+        _, results = attend(group, NNB, names, valid, queries, kv, kvt, pair_scr, x_out)
+        for one in group:
+            od_near[places[one]] = results[one]
+        return carry
+
+    far_steps(pairs, pass_on_far)
+    near_steps(pairs, pass_on)
+    take_share(jnp.int32(half))
     each_step(pairs, take_share)
-    each_step(pairs, finish)
-
-
-def attend_kernel(
-    blocks, neighbour_hbm, counts_hbm, qd, kv, kvt, od, totals,
-    neighbour, counts, starts, order, pair_scr, x_scr, load
-):
-    _, side = place_of()
-    half = blocks // 2
+    near_steps(pairs, take_near)
+    names_copy.wait()
+    counts_copy.wait()
+    lax.fori_loop(0, half // GROUP, near_group, 0)
+    far_steps(pairs, take_far)
+
+
+def attend(group, used, names, valid, qd, kv, kvt, pair_scr, x_out):
     scale = 1.0 / math.sqrt(E)
     exp_scale = scale * math.log2(math.e)
     low = lax.broadcasted_iota(jnp.int32, (BLK, 2 * E), 1) < E
     top = lax.broadcasted_iota(jnp.int32, (2 * E, BLK), 0) < E
+
+    def folded(array, op):
+        return op(array.reshape(BLK // 8, 8, BLK), axis=0)
+
+    spread, ahead = [], []
+    for one in group:
+        both = qd[one]
+        zero = jnp.zeros_like(both)
+        upper = jnp.where(low, both, zero)
+        lower = jnp.where(low, zero, both)
+        spread.append(jnp.concatenate([upper, lower], axis=0))
+        ahead.append(jnp.concatenate([upper, lower * jnp.asarray(scale, BF16)], axis=0))
+    highest = [None for _ in group]
+    for one in group:
+        keys = jnp.concatenate([kv[name] for name in names[one]], axis=0)
+        result = lax.dot_general(
+            keys, ahead[one], (((1,), (1,)), ((), ())), preferred_element_type=F32
+        ).reshape(used, BLK, 2 * BLK)
+        for slot in range(used):
+            pair_scr[one, slot] = result[slot]
+            part = folded(result[slot, :, :BLK], jnp.max)
+            if valid[one][slot] is not None:
+                part = jnp.where(valid[one][slot], part, -jnp.inf)
+            highest[one] = part if slot == 0 else jnp.maximum(highest[one], part)
+    highest = [jnp.max(part, axis=0, keepdims=True) for part in highest]
+    total = [jnp.zeros((8, BLK), F32) for _ in group]
+    delta = [jnp.zeros((8, BLK), F32) for _ in group]
+    for slot in range(used):
+        for one in group:
+            raised = jnp.exp2((pair_scr[one, slot, :, :BLK] - highest[one]) * exp_scale)
+            if valid[one][slot] is not None:
+                raised = jnp.where(valid[one][slot], raised, 0.0)
+            pair_scr[one, slot, :, :BLK] = raised
+            total[one] = total[one] + folded(raised, jnp.sum)
+            delta[one] = delta[one] + folded(raised * pair_scr[one, slot, :, BLK:], jnp.sum)
+    inverse = [1.0 / jnp.sum(part, axis=0, keepdims=True) for part in total]
+    delta = [jnp.sum(delta[one], axis=0, keepdims=True) * inverse[one] for one in group]
+    for slot in range(used):
+        for one in group:
+            probability = pair_scr[one, slot, :, :BLK] * inverse[one]
+            dscore = probability * (pair_scr[one, slot, :, BLK:] - delta[one])
+            x_out[one][slot] = jnp.concatenate(
+                [dscore.astype(BF16), probability.astype(BF16)], axis=1
+            )
+    results = []
+    for one in group:
+        rows = jnp.zeros((2 * E, 2 * BLK), F32)
+        for slot in range(0, used, 2):
+            if slot + 1 < used:
+                keys_t = jnp.concatenate(
+                    [kvt[names[one][slot]], kvt[names[one][slot + 1]]], axis=1
+                )
+                grads = jnp.concatenate([x_out[one][slot], x_out[one][slot + 1]], axis=0)
+            else:
+                keys_t = kvt[names[one][slot]]
+                grads = x_out[one][slot]
+            rows = rows + jnp.dot(keys_t, grads, preferred_element_type=F32)
+        results.append(jnp.where(top, rows[:, :BLK], rows[:, BLK:]).T.astype(BF16))
+    return spread, results
+
+
+def attend_kernel(
+    blocks, neighbour_hbm, counts_hbm, qd, kv, kvt, x_near, od_far, totals,
+    neighbour, counts, starts, order, pair_scr, x_scr, load
+):
+    owner, side = place_of()
+    pairs = blocks // 2
+    half = pairs // 2
+    near = lax.div(owner, half) * half
+    far = half - near
     names_copy = pltpu.make_async_copy(neighbour_hbm, neighbour, load.at[0])
     names_copy.start()
     counts_copy = pltpu.make_async_copy(counts_hbm, counts, load.at[1])
@@ -363,102 +477,68 @@
     names_copy.wait()
     counts_copy.wait()
 
-    def folded(array, op):
-        return op(array.reshape(BLK // 8, 8, BLK), axis=0)
+    def used_of(place):
+        return counts[2 * (far + place) + side]
 
     def sort_by_used():
         for used in range(NNB + 1):
             starts[used] = 0
         for place in range(half):
-            used = counts[2 * place + side]
+            used = used_of(place)
             starts[used - 1] = starts[used - 1] + 1
         for used in range(NNB - 1, -1, -1):
             starts[used] = starts[used] + starts[used + 1]
         for place in range(half):
-            used = counts[2 * place + side]
+            used = used_of(place)
             at = starts[used]
             order[at] = place
             starts[used] = at + 1
 
+    def add_up(names, x_of_block, spread):
+        used = len(names)
+        grads = x_of_block[:used].reshape(used * BLK, 2 * BLK)
+        added = jnp.dot(grads, spread, preferred_element_type=F32)
+        for slot in range(used):
+            totals[names[slot]] += added[slot * BLK : (slot + 1) * BLK]
+
     def rows_with(places, used):
         group = range(len(places))
-        blocks_now = [2 * place + side for place in places]
+        blocks_now = [2 * (far + place) + side for place in places]
         names = [[neighbour[slot, block] for slot in range(used)] for block in blocks_now]
-        valid = [[slot < counts[block] for slot in range(used)] for block in blocks_now]
-        spread, ahead = [], []
-        for place in places:
-            both = qd[place]
-            zero = jnp.zeros_like(both)
-            upper = jnp.where(low, both, zero)
-            lower = jnp.where(low, zero, both)
-            spread.append(jnp.concatenate([upper, lower], axis=0))
-            ahead.append(jnp.concatenate([upper, lower * jnp.asarray(scale, BF16)], axis=0))
-        highest = [None for _ in group]
-        for slot in range(used):
-            for one in group:
-                result = lax.dot_general(
-                    kv[names[one][slot]],
-                    ahead[one],
-                    (((1,), (1,)), ((), ())),
-                    preferred_element_type=F32,
-                )
-                pair_scr[one, slot] = result
-                part = folded(result[:, :BLK], jnp.max)
-                if one > 0 and slot > 0:
-                    part = jnp.where(valid[one][slot], part, -jnp.inf)
-                highest[one] = part if slot == 0 else jnp.maximum(highest[one], part)
-        highest = [jnp.max(part, axis=0, keepdims=True) for part in highest]
-        total = [jnp.zeros((8, BLK), F32) for _ in group]
-        delta = [jnp.zeros((8, BLK), F32) for _ in group]
-        for slot in range(used):
-            for one in group:
-                raised = jnp.exp2((pair_scr[one, slot, :, :BLK] - highest[one]) * exp_scale)
-                if one > 0 and slot > 0:
-                    raised = jnp.where(valid[one][slot], raised, 0.0)
-                pair_scr[one, slot, :, :BLK] = raised
-                total[one] = total[one] + folded(raised, jnp.sum)
-                delta[one] = delta[one] + folded(raised * pair_scr[one, slot, :, BLK:], jnp.sum)
-        inverse = [1.0 / jnp.sum(part, axis=0, keepdims=True) for part in total]
-        delta = [jnp.sum(delta[one], axis=0, keepdims=True) * inverse[one] for one in group]
-        for slot in range(used):
-            for one in group:
-                probability = pair_scr[one, slot, :, :BLK] * inverse[one]
-                dscore = probability * (pair_scr[one, slot, :, BLK:] - delta[one])
-                x_scr[one, slot] = jnp.concatenate(
-                    [dscore.astype(BF16), probability.astype(BF16)], axis=1
-                )
+        valid = [
+            [slot < counts[block] if one > 0 and slot > 0 else None for slot in range(used)]
+            for one, block in enumerate(blocks_now)
+        ]
+        x_out = [x_scr.at[one] for one in group]
+        queries = [qd[far + place] for place in places]
+        spread, results = attend(group, used, names, valid, queries, kv, kvt, pair_scr, x_out)
         for one in group:
-            rows = jnp.zeros((2 * E, 2 * BLK), F32)
-            for slot in range(0, used, 2):
-                if slot + 1 < used:
-                    keys_t = jnp.concatenate(
-                        [kvt[names[one][slot]], kvt[names[one][slot + 1]]], axis=1
-                    )
-                    grads = jnp.concatenate([x_scr[one, slot], x_scr[one, slot + 1]], axis=0)
-                else:
-                    keys_t = kvt[names[one][slot]]
-                    grads = x_scr[one, slot]
-                rows = rows + jnp.dot(keys_t, grads, preferred_element_type=F32)
-            od[places[one]] = jnp.where(top, rows[:, :BLK], rows[:, BLK:]).T.astype(BF16)
-        for slot in range(used):
-            for one in group:
-                totals[names[one][slot]] += jnp.dot(
-                    x_scr[one, slot], spread[one], preferred_element_type=F32
-                )
+            od_far[places[one]] = results[one]
+            add_up(names[one], x_out[one], spread[one])
 
     def one_group(turn, carry):
         places = [order[GROUP * turn + one] for one in range(GROUP)]
-        used_now = counts[2 * places[0] + side]
+        used_now = used_of(places[0])
         for used in range(1, NNB + 1):
             pl.when(used_now == used)(functools.partial(rows_with, places, used))
         return carry
 
+    def near_sums(place, carry):
+        low = lax.broadcasted_iota(jnp.int32, (BLK, 2 * E), 1) < E
+        both = qd[near + place]
+        zero = jnp.zeros_like(both)
+        spread = jnp.concatenate([jnp.where(low, both, zero), jnp.where(low, zero, both)], axis=0)
+        block = 2 * (near + place) + side
+        add_up([neighbour[slot, block] for slot in range(NNB)], x_near.at[place], spread)
+        return carry
+
     sort_by_used()
     lax.fori_loop(0, half // GROUP, one_group, 0)
+    lax.fori_loop(0, half, near_sums, 0)
 
 
 def collect_kernel(
-    pairs, od, totals, got_od, got_kv, other, shared, send_kv,
+    pairs, od_near, od_far, totals, got_od, got_kv, other, shared, send_kv,
     od_out, od_in, kv_out, kv_in, share_out, share_in,
 ):
     owner, side = place_of()
@@ -474,9 +554,9 @@
             device_id_type=MESH_ID,
         )
 
-    def od_copy(step, to, source):
+    def od_copy(array, step, to, source):
         return pltpu.make_async_remote_copy(
-            src_ref=od.at[to],
+            src_ref=array.at[lax.rem(to, pairs // 2)],
             dst_ref=got_od.at[source],
             send_sem=od_out.at[step],
             recv_sem=od_in.at[step],
@@ -501,9 +581,9 @@
     lax.fori_loop(0, pairs, narrow, 0)
     pl.semaphore_wait(barrier, pairs)
 
-    def start_all(step):
+    def start_all(array, step):
         to, _ = partners(pairs, owner, step)
-        od_copy(step, to, owner).start()
+        od_copy(array, step, to, owner).start()
         share_copy(step, to).start()
 
     def summed(place):
@@ -515,21 +595,23 @@
         send_kv[to] = summed(to)
         kv_copy(step, to, owner).start()
 
-    def finish(step):
+    def finish(array, step):
         to, source = partners(pairs, owner, step)
-        od_copy(step, owner, source).wait_recv()
+        od_copy(array, step, owner, source).wait_recv()
         kv_copy(step, owner, source).wait_recv()
-        od_copy(step, to, owner).wait_send()
+        od_copy(array, step, to, owner).wait_send()
         kv_copy(step, to, owner).wait_send()
         share_copy(step, to).wait_send()
 
-    each_step(pairs, start_all)
+    far_steps(pairs, functools.partial(start_all, od_far))
+    near_steps(pairs, functools.partial(start_all, od_near))
     share_copy(pairs // 2, owner).start()
     each_step(pairs, add_and_send)
     share_copy(pairs // 2, owner).wait_recv()
     got_kv[owner] = summed(owner)
-    got_od[owner] = od[owner]
-    each_step(pairs, finish)
+    got_od[owner] = od_near[lax.rem(owner, pairs // 2)]
+    far_steps(pairs, functools.partial(finish, od_far))
+    near_steps(pairs, functools.partial(finish, od_near))
     share_copy(pairs // 2, owner).wait_send()
 
 
@@ -559,49 +641,62 @@
     many = pltpu.SemaphoreType.DMA((pairs,))
     piece = (BLK, 2 * E)
     own_pieces = jax.ShapeDtypeStruct((pairs, *piece), BF16)
-    all_pieces = jax.ShapeDtypeStruct((blocks, *piece), BF16)
+    index_arrays = [
+        pltpu.SMEM(neighbour.shape[::-1], jnp.int32),
+        pltpu.SMEM(counts.shape, jnp.int32),
+    ]
     with jax.named_scope("spread_heads"):
-        qd, kv, kvt = pl.pallas_call(
+        qd, kv, kvt, x_near, od_near = pl.pallas_call(
             functools.partial(spread_kernel, pairs),
-            out_shape=tuple(pltpu.VMEM((count, *piece), BF16) for count in (pairs, blocks, blocks)),
-            in_specs=[in_hbm] * 4,
-            out_specs=(in_vmem,) * 3,
+            out_shape=(
+                pltpu.VMEM((pairs, *piece), BF16),
+                pltpu.VMEM((blocks, *piece), BF16),
+                pltpu.VMEM((blocks, *piece), BF16),
+                pltpu.VMEM((pairs // 2, NNB, BLK, 2 * BLK), BF16),
+                pltpu.VMEM((pairs // 2, *piece), BF16),
+            ),
+            in_specs=[in_hbm] * 6,
+            out_specs=(in_vmem,) * 5,
             scratch_shapes=[pltpu.VMEM((4, BLK, width), BF16)]
             + [pltpu.VMEM((pairs, *piece), BF16)] * 2
-            + [pltpu.SemaphoreType.DMA((4,))]
+            + index_arrays
+            + [pltpu.VMEM((GROUP, NNB, BLK, 2 * BLK), F32)]
+            + [pltpu.SemaphoreType.DMA((6,))]
             + [many] * 6,
             compiler_params=pltpu.CompilerParams(
                 collective_id=0, has_side_effects=True, vmem_limit_bytes=VMEM_BYTES
             ),
-        )(*map(left_in_hbm, (query, key, value, grad_out)))
+        )(*map(left_in_hbm, (query, key, value, grad_out, neighbour.T, counts)))
     with jax.named_scope("block_attention"):
-        od, totals = pl.pallas_call(
+        od_far, totals = pl.pallas_call(
             functools.partial(attend_kernel, blocks),
-            out_shape=(own_pieces, jax.ShapeDtypeStruct((blocks, *piece), F32)),
-            in_specs=[in_hbm] * 2 + [in_vmem] * 3,
+            out_shape=(
+                jax.ShapeDtypeStruct((pairs // 2, *piece), BF16),
+                jax.ShapeDtypeStruct((blocks, *piece), F32),
+            ),
+            in_specs=[in_hbm] * 2 + [in_vmem] * 4,
             out_specs=(in_vmem,) * 2,
             scratch_shapes=[
-                pltpu.SMEM(neighbour.shape[::-1], jnp.int32),
-                pltpu.SMEM(counts.shape, jnp.int32),
+                *index_arrays,
                 pltpu.SMEM((NNB + 1,), jnp.int32),
-                pltpu.SMEM((pairs,), jnp.int32),
+                pltpu.SMEM((pairs // 2,), jnp.int32),
                 pltpu.VMEM((GROUP, NNB, BLK, 2 * BLK), F32),
                 pltpu.VMEM((GROUP, NNB, BLK, 2 * BLK), BF16),
                 pltpu.SemaphoreType.DMA((2,)),
             ],
             compiler_params=pltpu.CompilerParams(vmem_limit_bytes=VMEM_BYTES),
-        )(left_in_hbm(neighbour.T), left_in_hbm(counts), qd, kv, kvt)
+        )(left_in_hbm(neighbour.T), left_in_hbm(counts), qd, kv, kvt, x_near)
     with jax.named_scope("collect_heads"):
         got_od, got_kv = pl.pallas_call(
             functools.partial(collect_kernel, pairs),
             out_shape=(own_pieces,) * 2,
-            in_specs=[in_vmem] * 2,
+            in_specs=[in_vmem] * 3,
             out_specs=(in_vmem,) * 2,
             scratch_shapes=[pltpu.VMEM((pairs, *piece), BF16)] * 3 + [many] * 6,
             compiler_params=pltpu.CompilerParams(
                 collective_id=1, has_side_effects=True, vmem_limit_bytes=VMEM_BYTES
             ),
-        )(od, totals)
+        )(od_near, od_far, totals)
     with jax.named_scope("join_heads"):
         return pl.pallas_call(
             functools.partial(join_kernel, pairs),
@@ -618,7 +713,7 @@
 
 def on_device(query, key, value, grad_out, neighbour, counts):
     devices = lax.axis_size("ctx") * lax.axis_size("head")
-    if devices == 2 * H and H % GROUP == 0 and query.shape == (BLK, H * E) and counts.shape[0] == devices:
+    if devices == 2 * H and H % (2 * GROUP) == 0 and query.shape == (BLK, H * E) and counts.shape[0] == devices:
         return on_device_whole(query, key, value, grad_out, neighbour, counts)
     return on_device_windowed(query, key, value, grad_out, neighbour, counts)
 

time: 72 us -> 71.9 us (level); the launches traced: 72.2 us -> 71.2 us
  Pallas kernels: 71.6 us -> 70.6 us
    pallas_call x2, Pallas kernels: 42.8 us -> 40.6 us  [the longest x1 31.5 us: on_device_whole(): pl.pallas_call(functools.partial(spread_kernel, pairs), out_shape=(pltpu....]
    pallas_call x1, Pallas kernels: 27.6 us -> 28.8 us  [on_device_whole(): pl.pallas_call(functools.partial(collect_kernel, pairs), out_shape=(own_p...]
where the time goes in v5:
time: 71.9 us; the launch traced here: 71.2 us
  Pallas kernels  70.6 us (98%)
    pallas_call x1, Pallas kernels, on_device_whole(): pl.pallas_call(functools.partial(spread_kernel, pairs), out_shape=(pltpu....  31.5 us
    pallas_call x1, Pallas kernels, on_device_whole(): pl.pallas_call(functools.partial(collect_kernel, pairs), out_shape=(own_p...  28.8 us
    pallas_call x1, Pallas kernels, on_device_whole(): pl.pallas_call(functools.partial(attend_kernel, blocks), out_shape=(jax.S...  9.11 us

profile of v5, /device:TPU:0, one launch (start us, length us, event | category | flops | bytes accessed | tf_op | source)
XLA Modules:
  0.0 71.2 jit_solution(968475651853271742)
XLA Ops:
  0.6 31.5 %spread_heads.1 = (bf16[16,128,128]{2,1,0:T(8,128)(2,1)S(1)}, bf16[32,128,128]{2,1,0:T(8,128)(2,1)S(1)}, bf16[32,128,128]{2,1,0:T(8,128)(2,1)S(1)}, bf16[8,8,128...) custom-call(bf16[128,1024]{1,0:T(8,128)(2,1)} %query.1, bf16[128,1024]{1,0:T(8,128)(2,1)} %key.1, ...), custom_call_target="tpu_custom_call" | custom-call | tf_op jit(solution)/shard_map/spread_heads/pallas_call | solution.py:649
  32.1 9.1 %block_attention.1 = (bf16[8,128,128]{2,1,0:T(8,128)(2,1)S(1)}, f32[32,128,128]{2,1,0:T(8,128)S(1)}) custom-call(s32[8,32]{1,0:T(8,128)} %bitcast.2, s32[32]{0:T(128)} %counts_hbm.3, bf16[16,128,128]{2,1,0:T(8,128)(2,1)S(1)} %get-tuple-element.14.qd, bf16[32,128,128]{2,1,0:T(8,128)(2,1)S(1)} %get-tuple-element.15.kv, ...), custom_call_target="tpu_custom_call" | custom-call | tf_op jit(solution)/shard_map/block_attention/pallas_call | solution.py:671
  41.2 28.8 %collect_heads.1 = (bf16[16,128,128]{2,1,0:T(8,128)(2,1)S(1)}, bf16[16,128,128]{2,1,0:T(8,128)(2,1)S(1)}) custom-call(bf16[8,128,128]{2,1,0:T(8,128)(2,1)S(1)} %get-tuple-element.13.od_near, bf16[8,128,128]{2,1,0:T(8,128)(2,1)S(1)} %get-tuple-element.18.od_far, f32[32,128,128]{2,1,0:T(8,128)S(1)} %get-tuple-element.19.totals), custom_call_target="tpu_custom_call" | custom-call | tf_op jit(solution)/shard_map/collect_heads/pallas_call | solution.py:690
  70.1 1.1 %join_heads.1 = (bf16[128,1024]{1,0:T(8,128)(2,1)}, bf16[128,1024]{1,0:T(8,128)(2,1)}, bf16[128,1024]{1,0:T(8,128)(2,1)}, bf16[128,1024]{1,0:T(8,128)(2,1)}) custom-call(bf16[16,128,128]{2,1,0:T(8,128)(2,1)S(1)} %get-tuple-element.20.got_od, bf16[16,128,128]{2,1,0:T(8,128)(2,1)S(1)} %get-tuple-element.21.got_kv), custom_call_target="tpu_custom_call" | custom-call | tf_op jit(solution)/shard_map/join_heads/pallas_call | solution.py:701

commit v6 on v5

--- a/solution.py
+++ b/solution.py
@@ -257,8 +257,8 @@
 
 
 def spread_kernel(
-    pairs, query, key, value, grad_out, neighbour_hbm, counts_hbm, qd, kv, kvt, x_near, od_near,
-    own_rows, send_qd, send_kv, neighbour, counts, pair_scr,
+    pairs, query, key, value, grad_out, neighbour_hbm, counts_hbm, qd, kv, kvt, sums_near, od_near,
+    own_rows, send_qd, send_kv, neighbour, counts, pair_scr, x_scr,
     load, qd_out, qd_in, kv_out, kv_in, share_out, share_in,
 ):
     owner, side = place_of()
@@ -372,10 +372,13 @@
             for block in blocks_now
         ]
         queries = [qd[near + place] for place in places]
-        x_out = [x_near.at[place] for place in places]
-        _, results = attend(group, NNB, names, valid, queries, kv, kvt, pair_scr, x_out)
+        x_out = [x_scr.at[one] for one in group]
+        spread, results = attend(group, NNB, names, valid, queries, kv, kvt, pair_scr, x_out)
         for one in group:
             od_near[places[one]] = results[one]
+            grads = x_scr[one].reshape(NNB * BLK, 2 * BLK)
+            added = jnp.dot(grads, spread[one], preferred_element_type=F32)
+            sums_near[places[one]] = added.reshape(NNB, BLK, 2 * E)
         return carry
 
     far_steps(pairs, pass_on_far)
@@ -456,7 +459,7 @@
 
 
 def attend_kernel(
-    blocks, neighbour_hbm, counts_hbm, qd, kv, kvt, x_near, od_far, totals,
+    blocks, neighbour_hbm, counts_hbm, qd, kv, kvt, sums_near, od_far, totals,
     neighbour, counts, starts, order, pair_scr, x_scr, load
 ):
     owner, side = place_of()
@@ -524,12 +527,13 @@
         return carry
 
     def near_sums(place, carry):
-        low = lax.broadcasted_iota(jnp.int32, (BLK, 2 * E), 1) < E
-        both = qd[near + place]
-        zero = jnp.zeros_like(both)
-        spread = jnp.concatenate([jnp.where(low, both, zero), jnp.where(low, zero, both)], axis=0)
         block = 2 * (near + place) + side
-        add_up([neighbour[slot, block] for slot in range(NNB)], x_near.at[place], spread)
+
+        def one_slot(slot, carry):
+            totals[neighbour[slot, block]] += sums_near[place, slot]
+            return carry
+
+        lax.fori_loop(0, counts[block], one_slot, 0)
         return carry
 
     sort_by_used()
@@ -646,13 +650,13 @@
         pltpu.SMEM(counts.shape, jnp.int32),
     ]
     with jax.named_scope("spread_heads"):
-        qd, kv, kvt, x_near, od_near = pl.pallas_call(
+        qd, kv, kvt, sums_near, od_near = pl.pallas_call(
             functools.partial(spread_kernel, pairs),
             out_shape=(
                 pltpu.VMEM((pairs, *piece), BF16),
                 pltpu.VMEM((blocks, *piece), BF16),
                 pltpu.VMEM((blocks, *piece), BF16),
-                pltpu.VMEM((pairs // 2, NNB, BLK, 2 * BLK), BF16),
+                pltpu.VMEM((pairs // 2, NNB, BLK, 2 * E), F32),
                 pltpu.VMEM((pairs // 2, *piece), BF16),
             ),
             in_specs=[in_hbm] * 6,
@@ -660,7 +664,7 @@
             scratch_shapes=[pltpu.VMEM((4, BLK, width), BF16)]
             + [pltpu.VMEM((pairs, *piece), BF16)] * 2
             + index_arrays
-            + [pltpu.VMEM((GROUP, NNB, BLK, 2 * BLK), F32)]
+            + [pltpu.VMEM((GROUP, NNB, BLK, 2 * BLK), kind) for kind in (F32, BF16)]
             + [pltpu.SemaphoreType.DMA((6,))]
             + [many] * 6,
             compiler_params=pltpu.CompilerParams(
@@ -685,7 +689,7 @@
                 pltpu.SemaphoreType.DMA((2,)),
             ],
             compiler_params=pltpu.CompilerParams(vmem_limit_bytes=VMEM_BYTES),
-        )(left_in_hbm(neighbour.T), left_in_hbm(counts), qd, kv, kvt, x_near)
+        )(left_in_hbm(neighbour.T), left_in_hbm(counts), qd, kv, kvt, sums_near)
     with jax.named_scope("collect_heads"):
         got_od, got_kv = pl.pallas_call(
             functools.partial(collect_kernel, pairs),

time: 71.9 us -> 70.2 us (0.976)
  Pallas kernels: 70.6 us -> 69.3 us
    pallas_call x1, Pallas kernels: 9.11 us -> 6.32 us  [on_device_whole(): pl.pallas_call(functools.partial(attend_kernel, blocks), out_shape=(jax.S...]
    pallas_call x1, Pallas kernels: 28.8 us -> 30.4 us  [on_device_whole(): pl.pallas_call(functools.partial(collect_kernel, pairs), out_shape=(own_p...]
where the time goes in v6:
time: 70.2 us; the launch traced here: 70 us
  Pallas kernels  69.3 us (99%)
    pallas_call x1, Pallas kernels, on_device_whole(): pl.pallas_call(functools.partial(spread_kernel, pairs), out_shape=(pltpu....  31.5 us
    pallas_call x1, Pallas kernels, on_device_whole(): pl.pallas_call(functools.partial(collect_kernel, pairs), out_shape=(own_p...  30.4 us
    pallas_call x1, Pallas kernels, on_device_whole(): pl.pallas_call(functools.partial(attend_kernel, blocks), out_shape=(jax.S...  6.32 us

profile of v6, /device:TPU:0, one launch (start us, length us, event | category | flops | bytes accessed | tf_op | source)
XLA Modules:
  0.0 70.0 jit_solution(13114544638130984410)
XLA Ops:
  0.6 31.5 %spread_heads.1 = (bf16[16,128,128]{2,1,0:T(8,128)(2,1)S(1)}, bf16[32,128,128]{2,1,0:T(8,128)(2,1)S(1)}, bf16[32,128,128]{2,1,0:T(8,128)(2,1)S(1)}, f32[8,8,128,...) custom-call(bf16[128,1024]{1,0:T(8,128)(2,1)} %query.1, bf16[128,1024]{1,0:T(8,128)(2,1)} %key.1, bf16[128,1024]{1,0:T(8,128)(2,1)} %value.1, ...), custom_call_target="tpu_custom_call" | custom-call | tf_op jit(solution)/shard_map/spread_heads/pallas_call | solution.py:653
  32.1 6.3 %block_attention.1 = (bf16[8,128,128]{2,1,0:T(8,128)(2,1)S(1)}, f32[32,128,128]{2,1,0:T(8,128)S(1)}) custom-call(s32[8,32]{1,0:T(8,128)} %bitcast.2, s32[32]{0:T(128)} %counts_hbm.3, bf16[16,128,128]{2,1,0:T(8,128)(2,1)S(1)} %get-tuple-element.14.qd, bf16[32,128,128]{2,1,0:T(8,128)(2,1)S(1)} %get-tuple-element.15.kv, ...), custom_call_target="tpu_custom_call" | custom-call | tf_op jit(solution)/shard_map/block_attention/pallas_call | solution.py:675
  38.5 30.4 %collect_heads.1 = (bf16[16,128,128]{2,1,0:T(8,128)(2,1)S(1)}, bf16[16,128,128]{2,1,0:T(8,128)(2,1)S(1)}) custom-call(bf16[8,128,128]{2,1,0:T(8,128)(2,1)S(1)} %get-tuple-element.13.od_near, bf16[8,128,128]{2,1,0:T(8,128)(2,1)S(1)} %get-tuple-element.18.od_far, f32[32,128,128]{2,1,0:T(8,128)S(1)} %get-tuple-element.19.totals), custom_call_target="tpu_custom_call" | custom-call | tf_op jit(solution)/shard_map/collect_heads/pallas_call | solution.py:694
  68.8 1.1 %join_heads.1 = (bf16[128,1024]{1,0:T(8,128)(2,1)}, bf16[128,1024]{1,0:T(8,128)(2,1)}, bf16[128,1024]{1,0:T(8,128)(2,1)}, bf16[128,1024]{1,0:T(8,128)(2,1)}) custom-call(bf16[16,128,128]{2,1,0:T(8,128)(2,1)S(1)} %get-tuple-element.20.got_od, bf16[16,128,128]{2,1,0:T(8,128)(2,1)S(1)} %get-tuple-element.21.got_kv), custom_call_target="tpu_custom_call" | custom-call | tf_op jit(solution)/shard_map/join_heads/pallas_call | solution.py:705

commit v7 on v6

--- a/solution.py
+++ b/solution.py
@@ -585,10 +585,13 @@
     lax.fori_loop(0, pairs, narrow, 0)
     pl.semaphore_wait(barrier, pairs)
 
-    def start_all(array, step):
+    def start_share(step):
+        to, _ = partners(pairs, owner, step)
+        share_copy(step, to).start()
+
+    def start_od(array, step):
         to, _ = partners(pairs, owner, step)
         od_copy(array, step, to, owner).start()
-        share_copy(step, to).start()
 
     def summed(place):
         return (totals[2 * place + side] + shared[place].astype(F32)).astype(BF16)
@@ -607,10 +610,13 @@
         kv_copy(step, to, owner).wait_send()
         share_copy(step, to).wait_send()
 
-    far_steps(pairs, functools.partial(start_all, od_far))
-    near_steps(pairs, functools.partial(start_all, od_near))
+    far_steps(pairs, start_share)
+    far_steps(pairs, functools.partial(start_od, od_far))
+    far_steps(pairs, add_and_send)
+    near_steps(pairs, start_share)
     share_copy(pairs // 2, owner).start()
-    each_step(pairs, add_and_send)
+    near_steps(pairs, functools.partial(start_od, od_near))
+    near_steps(pairs, add_and_send)
     share_copy(pairs // 2, owner).wait_recv()
     got_kv[owner] = summed(owner)
     got_od[owner] = od_near[lax.rem(owner, pairs // 2)]

time: 70.2 us -> 69.9 us (level)
  no operation moved by 1% of the time
where the time goes in v7:
time: 69.9 us; the launch traced here: 70.1 us
  Pallas kernels  69.4 us (99%)
    pallas_call x1, Pallas kernels, on_device_whole(): pl.pallas_call(functools.partial(spread_kernel, pairs), out_shape=(pltpu....  31.5 us
    pallas_call x1, Pallas kernels, on_device_whole(): pl.pallas_call(functools.partial(collect_kernel, pairs), out_shape=(own_p...  30.8 us
    pallas_call x1, Pallas kernels, on_device_whole(): pl.pallas_call(functools.partial(attend_kernel, blocks), out_shape=(jax.S...  5.99 us

profile of v7, /device:TPU:0, one launch (start us, length us, event | category | flops | bytes accessed | tf_op | source)
XLA Modules:
  0.0 70.1 jit_solution(2745413043642480348)
XLA Ops:
  0.6 31.5 %spread_heads.1 = (bf16[16,128,128]{2,1,0:T(8,128)(2,1)S(1)}, bf16[32,128,128]{2,1,0:T(8,128)(2,1)S(1)}, bf16[32,128,128]{2,1,0:T(8,128)(2,1)S(1)}, f32[8,8,128,...) custom-call(bf16[128,1024]{1,0:T(8,128)(2,1)} %query.1, bf16[128,1024]{1,0:T(8,128)(2,1)} %key.1, bf16[128,1024]{1,0:T(8,128)(2,1)} %value.1, ...), custom_call_target="tpu_custom_call" | custom-call | tf_op jit(solution)/shard_map/spread_heads/pallas_call | solution.py:659
  32.1 6.0 %block_attention.1 = (bf16[8,128,128]{2,1,0:T(8,128)(2,1)S(1)}, f32[32,128,128]{2,1,0:T(8,128)S(1)}) custom-call(s32[8,32]{1,0:T(8,128)} %bitcast.2, s32[32]{0:T(128)} %counts_hbm.3, bf16[16,128,128]{2,1,0:T(8,128)(2,1)S(1)} %get-tuple-element.14.qd, bf16[32,128,128]{2,1,0:T(8,128)(2,1)S(1)} %get-tuple-element.15.kv, ...), custom_call_target="tpu_custom_call" | custom-call | tf_op jit(solution)/shard_map/block_attention/pallas_call | solution.py:681
  38.1 30.8 %collect_heads.1 = (bf16[16,128,128]{2,1,0:T(8,128)(2,1)S(1)}, bf16[16,128,128]{2,1,0:T(8,128)(2,1)S(1)}) custom-call(bf16[8,128,128]{2,1,0:T(8,128)(2,1)S(1)} %get-tuple-element.13.od_near, bf16[8,128,128]{2,1,0:T(8,128)(2,1)S(1)} %get-tuple-element.18.od_far, f32[32,128,128]{2,1,0:T(8,128)S(1)} %get-tuple-element.19.totals), custom_call_target="tpu_custom_call" | custom-call | tf_op jit(solution)/shard_map/collect_heads/pallas_call | solution.py:700
  68.9 1.1 %join_heads.1 = (bf16[128,1024]{1,0:T(8,128)(2,1)}, bf16[128,1024]{1,0:T(8,128)(2,1)}, bf16[128,1024]{1,0:T(8,128)(2,1)}, bf16[128,1024]{1,0:T(8,128)(2,1)}) custom-call(bf16[16,128,128]{2,1,0:T(8,128)(2,1)S(1)} %get-tuple-element.20.got_od, bf16[16,128,128]{2,1,0:T(8,128)(2,1)S(1)} %get-tuple-element.21.got_kv), custom_call_target="tpu_custom_call" | custom-call | tf_op jit(solution)/shard_map/join_heads/pallas_call | solution.py:711
